TPU v7x, 128 devices: a whole 4x4x4 slice. The times are simulated.
128 devices in a mesh: dp: 8 (over x, core), seq: 16 (over y, z).
Axes of the slice: x: 4, y: 4, z: 4, core: 2. Of those that a mesh axis runs over, the one named last changes fastest.
Arguments:
- values: bfloat16 [8, 8192, 4096], P('dp', 'seq'), may hold values from -6 to 6
- gate_one: bfloat16 [8, 8192, 4096], P('dp', 'seq'), may hold values from -6 to 6
- gate_two: bfloat16 [8, 8192, 4096], P('dp', 'seq'), may hold values from -6 to 6
- gate_three: bfloat16 [8, 8192, 4096], P('dp', 'seq'), may hold values from -6 to 6
- genome_blocks: int32 [8, 4], P('dp'), may hold values from 1 to 32, 64 in all within a row
- short_taps: bfloat16 [7, 4096], replicated, may hold values from -2 to 2
- medium_taps: bfloat16 [128, 4096], P(None, 'dp'), may hold values from -0.5 to 0.5
- decay_rate: float32 [4096, 16], replicated, may hold values from 8.138021e-06 to 0.25, as said below
- residue: float32 [4096, 16], replicated, may hold values from -1.5 to 1.5
- long_skip: float32 [4096], replicated, may hold values from -1.75 to 1.75
Outputs:
- mixed: bfloat16 [8, 8192, 4096], P('dp', 'seq')
Inputs may be any that keep to these rules, and one draw needn't show every extreme that they name: `genome_blocks`: each row's 4 genome lengths, counted in blocks of 128 tokens, are positive and sum to 64; the longest is exactly 32. `decay_rate`: positive decay rates.
All inputs are finite; a program needn't handle non-finite values.
Results may differ from a plain program's by a relative error of at most 0.0085.
Values may be sent and summed in bfloat16 or wider, within the bound.
A program may use at most 256 MiB of HBM per device.

v0:
```python
import functools

import jax
import jax.numpy as jnp
import numpy as np
from jax import lax
from jax.experimental import pallas as pl
from jax.experimental.pallas import tpu as pltpu
from jax.sharding import PartitionSpec as P

SHORT_TAPS = 7
MED_TAPS = 128
BLOCK = 128
WIDE = 256
MODES = 16
LANES = 128
F32 = jnp.float32
BF16 = jnp.bfloat16
VMEM_LIMIT = 56 * 1024 * 1024


def transform_matrices():
    n = np.arange(2 * BLOCK)
    j = np.arange(BLOCK)
    angle = np.pi * (2 * j + 1)[:, None] * n[None] / (2 * BLOCK)
    forward = np.concatenate([np.cos(angle), -np.sin(angle)], axis=0)
    backward = np.concatenate([np.cos(angle).T, -np.sin(angle).T], axis=1) / BLOCK
    high = forward.astype(jnp.bfloat16)
    low = (forward - high.astype(np.float64)).astype(jnp.bfloat16)
    return high, low[:, :BLOCK], backward[BLOCK:].astype(jnp.bfloat16), backward[:BLOCK].astype(jnp.bfloat16)


def keep_scalars(genome_ref, position, count):
    begins = [jnp.int32(0)]
    for g in range(genome_ref.shape[1] - 1):
        begins.append(begins[-1] + genome_ref[0, g])
    keeps = []
    for b in range(count):
        block = position * count + b
        starts = functools.reduce(jnp.logical_or, [block == begin for begin in begins])
        keeps.append(jnp.where(starts, 0.0, 1.0).astype(F32))
    return keeps


def dot(a, b):
    return jnp.dot(a, b, preferred_element_type=F32)


def spectral_product(spec, taps_spec):
    wr, wi = spec[:BLOCK], spec[BLOCK:]
    tr, ti = taps_spec[:BLOCK], taps_spec[BLOCK:]
    return jnp.concatenate([(wr * tr - wi * ti).astype(BF16), (wr * ti + wi * tr).astype(BF16)], axis=0)


def kernel_first(genome_ref, values_ref, rim_ref, gate_ref, taps_ref, first_ref, window):
    count = values_ref.shape[0] // BLOCK
    keeps = keep_scalars(genome_ref, lax.axis_index("seq"), count)
    taps = taps_ref[...].astype(F32)
    for b in range(count):
        start = b * BLOCK
        for tile in range(WIDE // LANES):
            lanes = slice(tile * LANES, (tile + 1) * LANES)
            before = rim_ref[:, lanes] if b == 0 else values_ref[start - 16 : start, lanes]
            slot = b * (WIDE // LANES) + tile
            window[slot, 0:16] = before.astype(F32) * keeps[b]
            window[slot, 16 : 16 + BLOCK] = values_ref[start : start + BLOCK, lanes].astype(F32)
            total = window[slot, 16 : 16 + BLOCK] * taps[0:1, lanes]
            for k in range(1, SHORT_TAPS):
                total = total + window[slot, 16 - k : 16 - k + BLOCK] * taps[k : k + 1, lanes]
            gated = gate_ref[start : start + BLOCK, lanes].astype(F32) * total
            first_ref[start : start + BLOCK, lanes] = gated.astype(BF16)


def kernel_second(
    genome_ref, first_ref, halo_ref, gate_ref, taps_ref, rate_ref, fwd_ref, low_ref, back_ref, second_ref, local_ref
):
    count = first_ref.shape[0] // BLOCK
    keeps = keep_scalars(genome_ref, lax.axis_index("seq"), count)
    taps = taps_ref[...]
    taps_spec = dot(fwd_ref[:, :BLOCK], taps) + dot(low_ref[...], taps)
    for b in range(count):
        start = b * BLOCK
        before = halo_ref[...] if b == 0 else first_ref[start - BLOCK : start]
        spec = dot(fwd_ref[:, BLOCK:], first_ref[start : start + BLOCK]) + dot(fwd_ref[:, :BLOCK], before) * keeps[b]
        medium = dot(back_ref[...], spectral_product(spec, taps_spec))
        second_ref[start : start + BLOCK] = (gate_ref[start : start + BLOCK].astype(F32) * medium).astype(BF16)
    sub = lax.broadcasted_iota(jnp.int32, (1, 8, 1), 1).astype(F32)
    for tile in range(WIDE // LANES):
        lanes = slice(tile * LANES, (tile + 1) * LANES)
        rate = rate_ref[:, lanes][:, None, :]
        step = jnp.broadcast_to(jnp.exp(-8.0 * rate), (MODES, 8, LANES))
        weight = jnp.exp((sub - 8.0) * rate)
        for b in range(count):
            signal = second_ref[b * BLOCK : (b + 1) * BLOCK, lanes].astype(F32)
            acc = jnp.broadcast_to(signal[0:8][None], (MODES, 8, LANES))
            for j in range(1, BLOCK // 8):
                acc = acc * step + signal[8 * j : 8 * j + 8][None]
            local_ref[b, :, lanes] = jnp.sum(acc * weight, axis=1)


def kernel_mixed(
    genome_ref, second_ref, gate_ref, local_ref, incoming_ref, rate_ref, amplitude_ref, skip_ref, fwd_ref, low_ref, back_ref,
    mixed_ref, filt, carry,
):
    count = second_ref.shape[0] // BLOCK
    keeps = keep_scalars(genome_ref, lax.axis_index("seq"), count)
    sub = lax.broadcasted_iota(jnp.int32, (1, 8, 1), 1).astype(F32)
    for tile in range(WIDE // LANES):
        lanes = slice(tile * LANES, (tile + 1) * LANES)
        rate = rate_ref[:, lanes]
        amplitude = amplitude_ref[:, lanes]
        decay = jnp.exp(-float(BLOCK) * rate)
        rate = rate[:, None, :]
        step = jnp.broadcast_to(jnp.exp(-8.0 * rate), (MODES, 8, LANES))
        weight = amplitude[:, None, :] * jnp.exp(-sub * rate)
        part = weight
        for j in range(BLOCK // 8):
            filt[8 * j : 8 * j + 8, lanes] = jnp.sum(part, axis=0)
            part = part * step
        filt[0:1, lanes] = filt[0:1, lanes] + skip_ref[0:1, lanes]
        state = incoming_ref[:, lanes]
        for b in range(count):
            state = state * keeps[b]
            part = weight * state[:, None, :]
            for j in range(BLOCK // 8):
                carry[b * BLOCK + 8 * j : b * BLOCK + 8 * j + 8, lanes] = jnp.sum(part, axis=0)
                part = part * step
            if b < count - 1:
                state = decay * state + local_ref[b, :, lanes]
    taps = filt[...]
    high = taps.astype(BF16)
    low = (taps - high.astype(F32)).astype(BF16)
    taps_spec = dot(fwd_ref[:, :BLOCK], high) + dot(low_ref[...], high) + dot(fwd_ref[:, :BLOCK], low)
    for b in range(count):
        rows = slice(b * BLOCK, (b + 1) * BLOCK)
        spec = dot(fwd_ref[:, :BLOCK], second_ref[rows])
        total = dot(back_ref[...], spectral_product(spec, taps_spec)) + carry[rows]
        mixed_ref[rows] = (gate_ref[rows].astype(F32) * total).astype(BF16)


def chunked(rows):
    return pl.BlockSpec((rows, WIDE), lambda i: (0, i))


def whole(shape):
    return pl.BlockSpec(shape, lambda i: (0,) * len(shape))


def scan_states(total, rate, genome, parts, count):
    begin = jnp.cumsum(genome) - genome
    blocks = jnp.arange(parts * count, dtype=jnp.int32)
    keep = jnp.where(jnp.any(blocks[:, None] == begin[None], axis=1), 0.0, 1.0).astype(F32)
    through = jnp.prod(keep.reshape(parts, count), axis=1)
    decay = jnp.exp(-float(count * BLOCK) * rate)
    state = jnp.zeros_like(total[0])
    incoming = []
    for p in range(parts):
        incoming.append(state)
        state = through[p] * decay * state + total[p]
    return jnp.stack(incoming)


def body(values, gate_one, gate_two, gate_three, genome_blocks, short_taps, medium_taps, decay_rate, residue, long_skip):
    medium_full = lax.all_gather(medium_taps, "dp", axis=1, tiled=True)
    rows, channels = values.shape[1:]
    count = rows // BLOCK
    parts = lax.axis_size("seq")
    position = lax.axis_index("seq")
    pairs = [(i, i + 1) for i in range(parts - 1)]
    fwd, low, back_end, back_start = [jnp.asarray(m) for m in transform_matrices()]
    rate = decay_rate.T
    amplitude = residue.T * jnp.sqrt(-jnp.expm1(-2.0 * rate))
    signal = values[0]
    grid = (channels // WIDE,)
    params = pltpu.CompilerParams(vmem_limit_bytes=VMEM_LIMIT)
    smem = pl.BlockSpec(memory_space=pltpu.SMEM)

    rim = lax.ppermute(signal[rows - 16 :], "seq", pairs)
    first = pl.pallas_call(
        kernel_first,
        grid=grid,
        in_specs=[smem, chunked(rows), chunked(16), chunked(rows), chunked(SHORT_TAPS)],
        out_specs=chunked(rows),
        out_shape=jax.ShapeDtypeStruct((rows, channels), BF16),
        scratch_shapes=[pltpu.VMEM((count * (WIDE // LANES), 16 + BLOCK, LANES), F32)],
        compiler_params=params,
        name="first",
    )(genome_blocks, signal, rim, gate_one[0], short_taps)
    halo = lax.ppermute(first[rows - BLOCK :], "seq", pairs)
    second, local = pl.pallas_call(
        kernel_second,
        grid=grid,
        in_specs=[
            smem, chunked(rows), chunked(BLOCK), chunked(rows), chunked(BLOCK), chunked(MODES),
            whole(fwd.shape), whole(low.shape), whole(back_end.shape),
        ],
        out_specs=[chunked(rows), pl.BlockSpec((count, MODES, WIDE), lambda i: (0, 0, i))],
        out_shape=[
            jax.ShapeDtypeStruct((rows, channels), BF16),
            jax.ShapeDtypeStruct((count, MODES, channels), F32),
        ],
        compiler_params=params,
        name="second",
    )(genome_blocks, first, halo, gate_two[0], medium_full, rate, fwd, low, back_end)

    begin = jnp.cumsum(genome_blocks[0]) - genome_blocks[0]
    blocks = position * count + jnp.arange(count, dtype=jnp.int32)
    keep = jnp.where(jnp.any(blocks[:, None] == begin[None], axis=1), 0.0, 1.0).astype(F32)
    decay = jnp.exp(-float(BLOCK) * rate)
    total = local[0]
    for b in range(1, count):
        total = keep[b] * decay * total + local[b]
    width = channels // parts
    ends = lax.all_to_all(total.reshape(MODES, parts, width), "seq", split_axis=1, concat_axis=0, tiled=False)
    rate_part = lax.dynamic_slice_in_dim(rate, position * width, width, 1)
    incoming = scan_states(ends, rate_part, genome_blocks[0], parts, count)
    incoming = lax.all_to_all(incoming, "seq", split_axis=0, concat_axis=1, tiled=False).reshape(MODES, channels)

    mixed = pl.pallas_call(
        kernel_mixed,
        grid=grid,
        in_specs=[
            smem, chunked(rows), chunked(rows), pl.BlockSpec((count, MODES, WIDE), lambda i: (0, 0, i)),
            chunked(MODES), chunked(MODES), chunked(MODES), chunked(1),
            whole(fwd.shape), whole(low.shape), whole(back_start.shape),
        ],
        out_specs=chunked(rows),
        out_shape=jax.ShapeDtypeStruct((rows, channels), BF16),
        scratch_shapes=[pltpu.VMEM((BLOCK, WIDE), F32), pltpu.VMEM((rows, WIDE), F32)],
        compiler_params=params,
        name="mixed",
    )(
        genome_blocks, second, gate_three[0], local, incoming, rate, amplitude, long_skip[None],
        fwd, low, back_start,
    )
    return mixed[None]


def solution(mesh):
    return jax.shard_map(
        body,
        mesh=mesh,
        in_specs=(
            P("dp", "seq", None),
            P("dp", "seq", None),
            P("dp", "seq", None),
            P("dp", "seq", None),
            P("dp", None),
            P(),
            P(None, "dp"),
            P(),
            P(),
            P(),
        ),
        out_specs=P("dp", "seq", None),
        check_vma=False,
    )
```

profile of v0, /device:TPU:0, one launch (start us, length us, event | category | flops | bytes accessed | tf_op | source)
XLA Modules:
  0.0 168.8 jit_solution(14042937721401458407)
XLA Ops:
  6.5 0.7 all-gather.2.cloned.1.call-update
  7.3 0.9 slice_bitcast_fusion
  8.2 3.9 %collective-permute-start = (bf16[16,4096]{1,0:T(8,128)(2,1)S(1)}, bf16[16,4096]{1,0:T(8,128)(2,1)S(1)}, u32[]{:S(2)}, u32[]{:S(2)}) collective-permute-start(bf16[16,4096]{1,0:T(8,128)(2,1)S(1)} %slice_bitcast_fusion), channel_id=1, source_target_pairs={{0,1},{1,2},{2,3},{3,4},{4,5},{5,6},{6,7},{7,8},{8,9},{9,10},{10,1... | collective-permute-start | bytes 393224 | tf_op jit(solution)/shard_map/ppermute | solution.py:178
  12.1 2.7 %collective-permute-done.rim_ref = bf16[16,4096]{1,0:T(8,128)(2,1)S(1)} collective-permute-done((bf16[16,4096]{1,0:T(8,128)(2,1)S(1)}, bf16[16,4096]{1,0:T(8,128)(2,1)S(1)}, u32[]{:S(2)}, u32[]{:S(2)}) %collective-permute-start) | collective-permute-done | bytes 131104 | tf_op jit(solution)/shard_map/ppermute | solution.py:178
  15.5 13.6 %first.1.first_ref = bf16[512,4096]{1,0:T(8,128)(2,1)} custom-call(s32[1,4]{1,0:T(1,128)} %genome_ref.5, bf16[512,4096]{1,0:T(8,128)(2,1)} %bitcast.309, bf16[16,4096]{1,0:T(8,128)(2,1)} %copy-done.3, bf16[512,4096]{1,0:T(8,128)(2,1)} %bitcast.311, bf16[7,4096]{1,0:T(8,128)(2,1)} %taps_ref.1), custom_call_target="tpu_custom_call" | custom-call | tf_op jit(solution)/shard_map/first/pallas_call | solution.py:179
  29.1 1.3 slice.175
  30.4 4.4 %collective-permute-start.1 = (bf16[128,4096]{1,0:T(8,128)(2,1)S(1)}, bf16[128,4096]{1,0:T(8,128)(2,1)S(1)}, u32[]{:S(2)}, u32[]{:S(2)}) collective-permute-start(bf16[128,4096]{1,0:T(8,128)(2,1)S(1)} %slice.175), channel_id=1, source_target_pairs={{0,1},{1,2},{2,3},{3,4},{4,5},{5,6},{6,7},{7,8},{8,9},{9,10},{10,1... | collective-permute-start | bytes 3145736 | tf_op jit(solution)/shard_map/ppermute | solution.py:189
  35.3 0.7 fusion.27
  36.0 20.3 %collective-permute-done.1.halo_ref = bf16[128,4096]{1,0:T(8,128)(2,1)S(1)} collective-permute-done((bf16[128,4096]{1,0:T(8,128)(2,1)S(1)}, bf16[128,4096]{1,0:T(8,128)(2,1)S(1)}, u32[]{:S(2)}, u32[]{:S(2)}) %collective-permute-start.1) | collective-permute-done | bytes 1048608 | tf_op jit(solution)/shard_map/ppermute | solution.py:189
  56.4 1.0 copy-done.1
  57.4 27.4 %second.1 = (bf16[512,4096]{1,0:T(8,128)(2,1)}, f32[4,16,4096]{2,1,0:T(8,128)}) custom-call(s32[1,4]{1,0:T(1,128)} %genome_ref.5, bf16[512,4096]{1,0:T(8,128)(2,1)} %first.1.first_ref, bf16[128,4096]{1,0:T(8,128)(2,1)} %copy-done.1, bf16[512,4096]{1,0:T(8,128)(2,1)} %bitcast.312, bf16[128,4096]{1,0:T(8,128)(2,1)} %all-gather.2.cloned.1.call-done.taps_ref, ...), custom_call_target="tpu_custom_call" | custom-call | tf_op jit(solution)/shard_map/second/pallas_call | solution.py:190
  84.8 4.1 %bitcast_multiply_fusion = (f32[16,4096]{1,0:T(8,128)}, f32[16,4096]{1,0:T(8,128)S(1)}) fusion(f32[4096,16]{0,1:T(8,128)S(1)} %copy-done.2, f32[4096,16]{0,1:T(8,128)S(1)} %copy-done, f32[4,16,4096]{2,1,0:T(8,128)} %get-tuple-element.8.local_ref, f32[]{:T(128)} %bitcast.11, f32[]{:T(128)} %bitcast.10, f32[]{:T(128)} %bitcast.9), kind=kLoop, calls=%fused_computation | loop fusion | flops 851968 | bytes 2097164 | tf_op jit(solution)/shard_map/mul | solution.py:172
  88.9 0.9 copy.36
  89.8 9.9 %all-to-all-start = ((f32[1,16,16,256]{3,1,0,2:T(8,128)}), f32[1,16,16,256]{3,1,0,2:T(8,128)S(1)}, u32[]{:S(2)}, u32[]{:S(2)}) async-start(f32[1,16,16,256]{3,1,0,2:T(8,128)} %copy.36), calls=%async_computation | async-start | bytes 524288 | tf_op jit(solution)/shard_map/all_to_all | solution.py:214
  99.9 0.7 fusion.26
  100.6 7.5 %all-to-all-done = f32[1,16,16,256]{3,1,0,2:T(8,128)S(1)} async-done(((f32[1,16,16,256]{3,1,0,2:T(8,128)}), f32[1,16,16,256]{3,1,0,2:T(8,128)S(1)}, u32[]{:S(2)}, u32[]{:S(2)}) %all-to-all-start) | async-done | bytes 262176 | tf_op jit(solution)/shard_map/all_to_all | solution.py:214
  108.8 1.2 constant_dynamic-update-slice_fusion.13
  109.9 0.7 constant_dynamic-update-slice_fusion.12
  110.6 1.3 constant_dynamic-update-slice_fusion.11
  111.9 0.7 constant_dynamic-update-slice_fusion.10
  112.6 1.3 constant_dynamic-update-slice_fusion.9
  114.0 0.7 constant_dynamic-update-slice_fusion.8
  114.6 1.2 constant_dynamic-update-slice_fusion.7
  115.9 0.6 constant_dynamic-update-slice_fusion.6
  116.5 1.2 constant_dynamic-update-slice_fusion.5
  117.7 0.7 constant_dynamic-update-slice_fusion.4
  118.4 1.3 constant_dynamic-update-slice_fusion.3
  120.4 1.3 constant_dynamic-update-slice_fusion.1
  121.7 0.6 constant_dynamic-update-slice_fusion
  122.3 11.9 %all_to_all.30 = f32[16,16,1,256]{3,1,2,0:T(8,128)S(1)} all-to-all(f32[16,16,1,256]{3,1,2,0:T(8,128)S(1)} %bitcast.334), channel_id=1, replica_groups=mesh['dp'=8,'seq'=16] {'seq'}, dimensions={0} | all-to-all | bytes 524288 | tf_op jit(solution)/shard_map/all_to_all | solution.py:217
  134.3 0.7 copy.54
  135.0 26.9 %mixed.1 = bf16[512,4096]{1,0:T(8,128)(2,1)} custom-call(s32[1,4]{1,0:T(1,128)} %genome_ref.5, bf16[512,4096]{1,0:T(8,128)(2,1)} %get-tuple-element.7.second_ref, bf16[512,4096]{1,0:T(8,128)(2,1)} %bitcast.310, f32[4,16,4096]{2,1,0:T(8,128)} %get-tuple-element.8.local_ref, f32[16,4096]{1,0:T(8,128)} %bitcast.330, f32[16,4096]{1,0:T(8,128)} %bitcast.314, ...), custom_call_target="tpu_custom_call" | custom-call | tf_op jit(solution)/shard_map/mixed/pallas_call | solution.py:219
  (24 shorter events, 2.6 us)
Async XLA Ops:
  6.5 49.8 %all-gather.2.cloned.1.call-start = ((), (), s32[]{:S(2)}) async-start(), calls=%async_computation.2 | async-start | bytes 1179648 | tf_op jit(solution)/shard_map/all_gather | solution.py:164
  8.2 6.7 %collective-permute-start = (bf16[16,4096]{1,0:T(8,128)(2,1)S(1)}, bf16[16,4096]{1,0:T(8,128)(2,1)S(1)}, u32[]{:S(2)}, u32[]{:S(2)}) collective-permute-start(bf16[16,4096]{1,0:T(8,128)(2,1)S(1)} %slice_bitcast_fusion), channel_id=1, source_target_pairs={{0,1},{1,2},{2,3},{3,4},{4,5},{5,6},{6,7},{7,8},{8,9},{9,10},{10,1... | collective-permute-start | bytes 393224 | tf_op jit(solution)/shard_map/ppermute | solution.py:178
  14.8 0.6 copy-start.3
  15.5 19.4 %copy-start.4 = (s32[1,4]{1,0:T(1,128)S(1)}, s32[1,4]{1,0:T(1,128)}, u32[]{:S(2)}) copy-start(s32[1,4]{1,0:T(1,128)} %genome_ref.5) | copy-start | bytes 52
  30.4 25.9 %collective-permute-start.1 = (bf16[128,4096]{1,0:T(8,128)(2,1)S(1)}, bf16[128,4096]{1,0:T(8,128)(2,1)S(1)}, u32[]{:S(2)}, u32[]{:S(2)}) collective-permute-start(bf16[128,4096]{1,0:T(8,128)(2,1)S(1)} %slice.175), channel_id=1, source_target_pairs={{0,1},{1,2},{2,3},{3,4},{4,5},{5,6},{6,7},{7,8},{8,9},{9,10},{10,1... | collective-permute-start | bytes 3145736 | tf_op jit(solution)/shard_map/ppermute | solution.py:189
  56.4 1.0 copy-start.1
  57.4 27.4 %copy-start = (f32[4096,16]{0,1:T(8,128)S(1)}, f32[4096,16]{0,1:T(8,128)}, u32[]{:S(2)}) copy-start(f32[4096,16]{0,1:T(8,128)} %param.21) | copy-start | bytes 786436
  57.4 27.4 %copy-start.2 = (f32[4096,16]{0,1:T(8,128)S(1)}, f32[4096,16]{0,1:T(8,128)}, u32[]{:S(2)}) copy-start(f32[4096,16]{0,1:T(8,128)} %param.22) | copy-start | bytes 786436
  89.8 18.4 %all-to-all-start = ((f32[1,16,16,256]{3,1,0,2:T(8,128)}), f32[1,16,16,256]{3,1,0,2:T(8,128)S(1)}, u32[]{:S(2)}, u32[]{:S(2)}) async-start(f32[1,16,16,256]{3,1,0,2:T(8,128)} %copy.36), calls=%async_computation | async-start | bytes 524288 | tf_op jit(solution)/shard_map/all_to_all | solution.py:214
Sparse Core Ops, SparseCore 0:
  9.0 25.7 all-gather.1
where the time goes:
time: 170 us; the launch traced here: 169 us
  Pallas kernels  68 us (40%)
  waiting for transfers between devices  31.3 us (18%)
  other arithmetic  18.7 us (11%)
  starting transfers between devices  18.2 us (11%)
  between operations  13.6 us (8%)
  blocking collectives  11.9 us (7%)
  local copies, waits for them, and re-layouts  7.03 us (4%)
    pallas_call x1, Pallas kernels, body(): pl.pallas_call(kernel_second, grid=grid, in_specs=[smem, chunked(rows), c...  27.4 us
    pallas_call x1, Pallas kernels, body(): pl.pallas_call(kernel_mixed, grid=grid, in_specs=[smem, chunked(rows), ch...  26.9 us
    ppermute x1, waiting for transfers between devices, body(): halo = lax.ppermute(first[rows - BLOCK:], 'seq', pairs)  20.3 us
    pallas_call x1, Pallas kernels, body(): pl.pallas_call(kernel_first, grid=grid, in_specs=[smem, chunked(rows), ch...  13.6 us
    unnamed x14, other arithmetic  13.4 us
    all_to_all x1, blocking collectives, body(): lax.all_to_all(incoming, 'seq', split_axis=0, concat_axis=1, tiled=False)  11.9 us
    all_to_all x1, starting transfers between devices, body(): lax.all_to_all(total.reshape(MODES, parts, width), 'seq', split_axis=1, c...  9.88 us
    all_to_all x1, waiting for transfers between devices, body(): lax.all_to_all(total.reshape(MODES, parts, width), 'seq', split_axis=1, c...  7.52 us
  transfers between devices with their start and end apart: 4, of which 3 were waited for; matrix products, arithmetic and copies ran while one was open for 3% of the time, Pallas kernels for 8%

commit v1 on v0

v1 whole, which is shorter than its diff:
```python
import functools

import jax
import jax.numpy as jnp
import numpy as np
from jax import lax
from jax.experimental import pallas as pl
from jax.experimental.pallas import tpu as pltpu
from jax.sharding import PartitionSpec as P

SHORT_TAPS = 7
MED_TAPS = 128
BLOCK = 128
WIDE = 512
MODES = 16
LANES = 128
F32 = jnp.float32
BF16 = jnp.bfloat16
VMEM_LIMIT = 58 * 1024 * 1024


def transform_matrices():
    n = np.arange(2 * BLOCK)
    j = np.arange(BLOCK)
    angle = np.pi * (2 * j + 1)[:, None] * n[None] / (2 * BLOCK)
    forward = np.concatenate([np.cos(angle), -np.sin(angle)], axis=0)
    backward = np.concatenate([np.cos(angle).T, -np.sin(angle).T], axis=1) / BLOCK
    high = forward.astype(jnp.bfloat16)
    low = (forward - high.astype(np.float64)).astype(jnp.bfloat16)
    return high, low[:, :BLOCK], backward[BLOCK:].astype(jnp.bfloat16), backward[:BLOCK].astype(jnp.bfloat16)


def keep_scalars(genome_ref, position, count):
    begins = [jnp.int32(0)]
    for g in range(genome_ref.shape[1] - 1):
        begins.append(begins[-1] + genome_ref[0, g])
    keeps = []
    for b in range(count):
        block = position * count + b
        starts = functools.reduce(jnp.logical_or, [block == begin for begin in begins])
        keeps.append(jnp.where(starts, 0.0, 1.0).astype(F32))
    return keeps


def dot(a, b):
    return jnp.dot(a, b, preferred_element_type=F32)


def staged(fwd_of, signal_of, back, taps_spec, spec, product, blocks):
    for b in blocks:
        spec[b] = dot(fwd_of(b), signal_of(b))
    for b in blocks:
        for r in range(0, BLOCK, 16):
            re, im = slice(r, r + 16), slice(BLOCK + r, BLOCK + r + 16)
            wr, wi, tr, ti = spec[b, re], spec[b, im], taps_spec(re), taps_spec(im)
            product[b, re] = (wr * tr - wi * ti).astype(BF16)
            product[b, im] = (wr * ti + wi * tr).astype(BF16)
    return [(b, dot(back, product[b])) for b in blocks]


def lane_window(i, width):
    return pl.ds(pl.multiple_of(i * width, width), width)


def short_block(values, before, gate, taps, keep, window, first, rows, i):
    for tile in range(WIDE // LANES):
        lanes = pl.ds(pl.multiple_of(i * WIDE + tile * LANES, LANES), LANES)
        window[tile, 0:16] = before(lanes).astype(F32) * keep
        window[tile, 16 : 16 + BLOCK] = values[rows, lanes].astype(F32)
        weights = taps[:, lanes].astype(F32)
        total = window[tile, 16 : 16 + BLOCK] * weights[0:1]
        for k in range(1, SHORT_TAPS):
            total = total + window[tile, 16 - k : 16 - k + BLOCK] * weights[k : k + 1]
        first[rows, lanes] = (gate[rows, lanes].astype(F32) * total).astype(BF16)


def block_states(second, rate_ref, local, blocks, i):
    sub = lax.broadcasted_iota(jnp.int32, (1, 8, 1), 1).astype(F32)
    for tile in range(WIDE // LANES):
        lanes = pl.ds(pl.multiple_of(i * WIDE + tile * LANES, LANES), LANES)
        rate = rate_ref[:, lanes][:, None, :]
        step = jnp.broadcast_to(jnp.exp(-8.0 * rate), (MODES, 8, LANES))
        weight = jnp.exp((sub - 8.0) * rate)
        for b in blocks:
            signal = second[b * BLOCK : (b + 1) * BLOCK, lanes].astype(F32)
            acc = jnp.broadcast_to(signal[0:8][None], (MODES, 8, LANES))
            for j in range(1, BLOCK // 8):
                acc = acc * step + signal[8 * j : 8 * j + 8][None]
            local[b, :, lanes] = jnp.sum(acc * weight, axis=1)


def kernel_states(
    genome_ref, values_hbm, gate_one_hbm, gate_two_hbm, short_ref, taps_ref, rate_ref, fwd_ref, low_ref, back_ref,
    second_out, local_out, incoming_out,
    values, gate_one, gate_two, first, second, halo, rim, taps_full, taps_spec, local, ends_own, ends, entering,
    fwd_keep, window, spec, product,
    load_sem, store_sem, rim_sem, halo_send, halo_recv, taps_send, taps_recv, ends_send, ends_recv, enter_send, enter_recv,
):
    rows, channels = values.shape
    count = rows // BLOCK
    chunks = channels // WIDE
    parts = lax.axis_size("seq")
    width = channels // parts
    per_chunk = WIDE // width
    dps = lax.axis_size("dp")
    chips = dps // 2
    seq = lax.axis_index("seq")
    dp = lax.axis_index("dp")
    chip, core = dp // 2, dp % 2
    twin = chip * 2 + (1 - core)
    following = lax.rem(seq + 1, parts)
    keeps = keep_scalars(genome_ref, seq, count)
    tail = rows - BLOCK

    def remote(src, dst, send, recv, dp_to, seq_to):
        return pltpu.make_async_remote_copy(
            src_ref=src, dst_ref=dst, send_sem=send, recv_sem=recv,
            device_id=(dp_to, seq_to), device_id_type=pl.DeviceIdType.MESH,
        )

    loads = []
    for src, dst, part in (
        (values_hbm, values, slice(tail - 16, rows)),
        (gate_one_hbm, gate_one, slice(tail, rows)),
        (values_hbm, values, slice(0, tail - 16)),
        (gate_one_hbm, gate_one, slice(0, tail)),
        (gate_two_hbm, gate_two, slice(0, rows)),
    ):
        copy = pltpu.make_async_copy(src.at[part], dst.at[part], load_sem.at[len(loads)])
        copy.start()
        loads.append(copy)

    barrier = pltpu.get_barrier_semaphore()
    peers = 0
    for k in range(1, parts):
        pl.semaphore_signal(
            barrier, inc=1, device_id=(dp, lax.rem(seq + k, parts)), device_id_type=pl.DeviceIdType.MESH
        )
        peers += 1
    for k in range(1, chips):
        pl.semaphore_signal(
            barrier, inc=1, device_id=(lax.rem(chip + k, chips) * 2 + core, seq), device_id_type=pl.DeviceIdType.MESH
        )
        peers += 1
    pl.semaphore_signal(barrier, inc=1, device_id=(twin, seq), device_id_type=pl.DeviceIdType.MESH)
    pl.semaphore_wait(barrier, peers + 1)

    rim_copy = remote(values_hbm.at[slice(rows - 16, rows)], rim, rim_sem.at[0], rim_sem.at[1], dp, following)
    rim_copy.start()

    def taps_copy(slot, index, src, dp_to):
        return remote(src, taps_full.at[slot], taps_send.at[index], taps_recv.at[slot], dp_to, seq)

    taps_own = pltpu.make_async_copy(taps_ref, taps_full.at[dp], taps_recv.at[dp])
    taps_own.start()
    taps_copies = [taps_copy(dp, k - 1, taps_ref, lax.rem(chip + k, chips) * 2 + core) for k in range(1, chips)]
    taps_copies.append(taps_copy(dp, chips - 1, taps_ref, twin))
    for copy in taps_copies:
        copy.start()

    loads[0].wait()
    loads[1].wait()

    def halo_copy(i):
        lanes = lane_window(i, WIDE)
        return remote(
            first.at[slice(tail, rows), lanes], halo.at[:, lanes], halo_send.at[i], halo_recv.at[i], dp, following
        )

    def tail_step(i, carry):
        short_block(
            values, lambda lanes: values[tail - 16 : tail, lanes], gate_one, short_ref, keeps[count - 1], window, first,
            slice(tail, rows), i,
        )
        halo_copy(i).start()
        return carry

    lax.fori_loop(0, chunks, tail_step, 0)

    for b in range(count):
        column = lax.broadcasted_iota(jnp.int32, fwd_ref.shape, 1)
        matrix = fwd_ref[...].astype(F32)
        fwd_keep[b] = jnp.where(column < BLOCK, matrix * keeps[b], matrix).astype(BF16)

    loads[2].wait()
    loads[3].wait()
    rim_copy.wait()

    def first_step(i, carry):
        for b in range(count - 1):
            start = b * BLOCK
            if b == 0:
                before = lambda lanes: rim[:, lanes]
            else:
                before = lambda lanes, start=start: values[start - 16 : start, lanes]
            short_block(values, before, gate_one, short_ref, keeps[b], window, first, slice(start, start + BLOCK), i)
        return carry

    lax.fori_loop(0, chunks, first_step, 0)

    forwards = []
    for k in range(1, chips):
        source = lax.rem(chip + k, chips) * 2 + core
        taps_copy(source, k - 1, taps_ref, source).wait_recv()
        copy = taps_copy(source, chips - 1 + k, taps_full.at[source], twin)
        copy.start()
        forwards.append(copy)
    taps_own.wait()
    for k in range(chips):
        source = lax.rem(chip + k, chips) * 2 + (1 - core)
        taps_copy(source, chips - 1, taps_ref, twin).wait_recv()
    loads[4].wait()

    def second_step(i, carry):
        lanes = lane_window(i, WIDE)
        taps = taps_full[i]
        taps_spec[:, lanes] = dot(fwd_ref[:, :BLOCK], taps) + dot(low_ref[...], taps)
        blocks = range(1, count)
        for b, medium in staged(
            lambda b: fwd_keep[b], lambda b: first[(b - 1) * BLOCK : (b + 1) * BLOCK, lanes], back_ref[...],
            lambda part: taps_spec[part, lanes], spec, product, blocks,
        ):
            part = slice(b * BLOCK, (b + 1) * BLOCK)
            second[part, lanes] = (gate_two[part, lanes].astype(F32) * medium).astype(BF16)
        block_states(second, rate_ref, local, blocks, i)
        return carry

    lax.fori_loop(0, chunks, second_step, 0)
    late = slice(BLOCK, rows)
    store_late = pltpu.make_async_copy(second.at[late], second_out.at[late], store_sem.at[0])
    store_late.start()

    def ends_copy(part):
        return remote(ends_own.at[part], ends.at[seq], ends_send.at[part], ends_recv.at[seq], dp, part)

    def opening_step(i, carry):
        lanes = lane_window(i, WIDE)
        halo_copy(i).wait_recv()
        spec[0] = dot(fwd_keep[0, :, :BLOCK], halo[:, lanes]) + dot(fwd_keep[0, :, BLOCK:], first[0:BLOCK, lanes])
        for r in range(0, BLOCK, 16):
            re, im = slice(r, r + 16), slice(BLOCK + r, BLOCK + r + 16)
            wr, wi, tr, ti = spec[0, re], spec[0, im], taps_spec[re, lanes], taps_spec[im, lanes]
            product[0, re] = (wr * tr - wi * ti).astype(BF16)
            product[0, im] = (wr * ti + wi * tr).astype(BF16)
        medium = dot(back_ref[...], product[0])
        second[0:BLOCK, lanes] = (gate_two[0:BLOCK, lanes].astype(F32) * medium).astype(BF16)
        block_states(second, rate_ref, local, range(1), i)
        decay = jnp.exp(-float(BLOCK) * rate_ref[:, lanes])
        total = local[0, :, lanes]
        for b in range(1, count):
            total = keeps[b] * decay * total + local[b, :, lanes]
        for h in range(per_chunk):
            part = i * per_chunk + h
            ends_own[part] = total[:, h * width : (h + 1) * width]

            @pl.when(part != seq)
            def _():
                ends_copy(part).start()

            @pl.when(part == seq)
            def _():
                ends[part] = total[:, h * width : (h + 1) * width]

        return carry

    lax.fori_loop(0, chunks, opening_step, 0)
    early = slice(0, BLOCK)
    store_early = pltpu.make_async_copy(second.at[early], second_out.at[early], store_sem.at[1])
    store_early.start()
    store_local = pltpu.make_async_copy(local, local_out, store_sem.at[2])
    store_local.start()

    def arrival(k, carry):
        source = lax.rem(seq + k, parts)
        remote(ends_own.at[source], ends.at[source], ends_send.at[source], ends_recv.at[source], dp, source).wait_recv()
        return carry

    lax.fori_loop(1, parts, arrival, 0)

    begins = [jnp.int32(0)]
    for g in range(genome_ref.shape[1] - 1):
        begins.append(begins[-1] + genome_ref[0, g])
    decay = jnp.exp(-float(rows) * rate_ref[:, lane_window(seq, width)])

    def enter_copy(p):
        return remote(entering.at[p], incoming_out.at[seq], enter_send.at[p], enter_recv.at[seq], dp, p)

    def scan_step(p, state):
        entering[p] = state

        @pl.when(p != seq)
        def _():
            enter_copy(p).start()

        through = jnp.float32(1.0)
        for b in range(count):
            for begin in begins:
                through = jnp.where(p * count + b == begin, 0.0, through)
        return through * decay * state + ends[p]

    lax.fori_loop(0, parts, scan_step, jnp.zeros((MODES, width), F32))
    enter_own = pltpu.make_async_copy(entering.at[seq], incoming_out.at[seq], store_sem.at[3])
    enter_own.start()

    def departures(k, carry):
        other = lax.rem(seq + k, parts)
        ends_copy(other).wait_send()
        enter_copy(other).wait_send()
        remote(entering.at[other], incoming_out.at[other], enter_send.at[other], enter_recv.at[other], dp, other).wait_recv()
        return carry

    lax.fori_loop(1, parts, departures, 0)

    def halo_sent(i, carry):
        halo_copy(i).wait_send()
        return carry

    lax.fori_loop(0, chunks, halo_sent, 0)
    for copy in taps_copies + forwards:
        copy.wait_send()
    for copy in (store_late, store_early, store_local, enter_own):
        copy.wait()


def kernel_mixed(
    genome_ref, second_ref, gate_ref, local_ref, incoming_ref, rate_ref, amplitude_ref, skip_ref, fwd_ref, low_ref, back_ref,
    mixed_ref, filt, carry, taps_spec, spec, product,
):
    count = second_ref.shape[0] // BLOCK
    keeps = keep_scalars(genome_ref, lax.axis_index("seq"), count)
    sub = lax.broadcasted_iota(jnp.int32, (1, 8, 1), 1).astype(F32)
    pieces, _, width = incoming_ref.shape
    for tile in range(WIDE // LANES):
        lanes = slice(tile * LANES, (tile + 1) * LANES)
        rate = rate_ref[:, lanes]
        decay = jnp.exp(-float(BLOCK) * rate)
        rate = rate[:, None, :]
        step = jnp.broadcast_to(jnp.exp(-8.0 * rate), (MODES, 8, LANES))
        weight = amplitude_ref[:, lanes][:, None, :] * jnp.exp(-sub * rate)
        part = weight
        for j in range(BLOCK // 8):
            filt[8 * j : 8 * j + 8, lanes] = jnp.sum(part, axis=0)
            part = part * step
        filt[0:1, lanes] = filt[0:1, lanes] + skip_ref[0:1, lanes]
    taps = filt[...]
    high = taps.astype(BF16)
    low = (taps - high.astype(F32)).astype(BF16)
    taps_spec[...] = dot(fwd_ref[:, :BLOCK], high) + dot(low_ref[...], high) + dot(fwd_ref[:, :BLOCK], low)
    for b in range(count):
        spec[b] = dot(fwd_ref[:, :BLOCK], second_ref[b * BLOCK : (b + 1) * BLOCK])
    for tile in range(WIDE // LANES):
        lanes = slice(tile * LANES, (tile + 1) * LANES)
        rate = rate_ref[:, lanes]
        decay = jnp.exp(-float(BLOCK) * rate)
        rate = rate[:, None, :]
        step = jnp.broadcast_to(jnp.exp(-8.0 * rate), (MODES, 8, LANES))
        weight = amplitude_ref[:, lanes][:, None, :] * jnp.exp(-sub * rate)
        piece, offset = tile * LANES // width, tile * LANES % width
        state = incoming_ref[piece, :, offset : offset + LANES]
        for b in range(count):
            state = state * keeps[b]
            part = weight * state[:, None, :]
            for j in range(BLOCK // 8):
                carry[b * BLOCK + 8 * j : b * BLOCK + 8 * j + 8, lanes] = jnp.sum(part, axis=0)
                part = part * step
            if b < count - 1:
                state = decay * state + local_ref[b, :, lanes]
    for b in range(count):
        for r in range(0, BLOCK, 16):
            re, im = slice(r, r + 16), slice(BLOCK + r, BLOCK + r + 16)
            wr, wi, tr, ti = spec[b, re], spec[b, im], taps_spec[re], taps_spec[im]
            product[b, re] = (wr * tr - wi * ti).astype(BF16)
            product[b, im] = (wr * ti + wi * tr).astype(BF16)
    for b in range(count):
        rows = slice(b * BLOCK, (b + 1) * BLOCK)
        total = dot(back_ref[...], product[b]) + carry[rows]
        mixed_ref[rows] = (gate_ref[rows].astype(F32) * total).astype(BF16)


def chunked(rows):
    return pl.BlockSpec((rows, WIDE), lambda i: (0, i))


def whole(shape):
    return pl.BlockSpec(shape, lambda i: (0,) * len(shape))


def body(values, gate_one, gate_two, gate_three, genome_blocks, short_taps, medium_taps, decay_rate, residue, long_skip):
    rows, channels = values.shape[1:]
    count = rows // BLOCK
    parts = lax.axis_size("seq")
    dps = lax.axis_size("dp")
    width = channels // parts
    chunks = channels // WIDE
    fwd, low, back_end, back_start = [jnp.asarray(m) for m in transform_matrices()]
    rate = decay_rate.T
    amplitude = residue.T * jnp.sqrt(-jnp.expm1(-2.0 * rate))
    smem = pl.BlockSpec(memory_space=pltpu.SMEM)
    vmem = pl.BlockSpec(memory_space=pltpu.VMEM)
    hbm = pl.BlockSpec(memory_space=pl.ANY)
    stream = pltpu.VMEM((rows, channels), BF16)
    dma = pltpu.SemaphoreType.DMA

    second, local, incoming = pl.pallas_call(
        kernel_states,
        in_specs=[smem, hbm, hbm, hbm, vmem, vmem, vmem, vmem, vmem, vmem],
        out_specs=[hbm, hbm, hbm],
        out_shape=[
            jax.ShapeDtypeStruct((rows, channels), BF16),
            jax.ShapeDtypeStruct((count, MODES, channels), F32),
            jax.ShapeDtypeStruct((parts, MODES, width), F32),
        ],
        scratch_shapes=[
            stream, stream, stream, stream, stream,
            pltpu.VMEM((BLOCK, channels), BF16),
            pltpu.VMEM((16, channels), BF16),
            pltpu.VMEM((dps, BLOCK, WIDE), BF16),
            pltpu.VMEM((2 * BLOCK, channels), F32),
            pltpu.VMEM((count, MODES, channels), F32),
            pltpu.VMEM((parts, MODES, width), F32),
            pltpu.VMEM((parts, MODES, width), F32),
            pltpu.VMEM((parts, MODES, width), F32),
            pltpu.VMEM((count, 2 * BLOCK, 2 * BLOCK), BF16),
            pltpu.VMEM((WIDE // LANES, 16 + BLOCK, LANES), F32),
            pltpu.VMEM((count, 2 * BLOCK, WIDE), F32),
            pltpu.VMEM((count, 2 * BLOCK, WIDE), BF16),
            dma((5,)), dma((4,)), dma((2,)), dma((chunks,)), dma((chunks,)), dma((dps,)), dma((dps,)),
            dma((parts,)), dma((parts,)), dma((parts,)), dma((parts,)),
        ],
        compiler_params=pltpu.CompilerParams(
            vmem_limit_bytes=VMEM_LIMIT, collective_id=0, has_side_effects=True
        ),
        name="states",
    )(genome_blocks, values[0], gate_one[0], gate_two[0], short_taps, medium_taps, rate, fwd, low, back_end)

    per_chunk = WIDE // width
    mixed = pl.pallas_call(
        kernel_mixed,
        grid=(chunks,),
        in_specs=[
            smem, chunked(rows), chunked(rows), pl.BlockSpec((count, MODES, WIDE), lambda i: (0, 0, i)),
            pl.BlockSpec((per_chunk, MODES, width), lambda i: (i, 0, 0)),
            chunked(MODES), chunked(MODES), chunked(1),
            whole(fwd.shape), whole(low.shape), whole(back_start.shape),
        ],
        out_specs=chunked(rows),
        out_shape=jax.ShapeDtypeStruct((rows, channels), BF16),
        scratch_shapes=[
            pltpu.VMEM((BLOCK, WIDE), F32),
            pltpu.VMEM((rows, WIDE), F32),
            pltpu.VMEM((2 * BLOCK, WIDE), F32),
            pltpu.VMEM((count, 2 * BLOCK, WIDE), F32),
            pltpu.VMEM((count, 2 * BLOCK, WIDE), BF16),
        ],
        compiler_params=pltpu.CompilerParams(vmem_limit_bytes=VMEM_LIMIT),
        name="mixed",
    )(genome_blocks, second, gate_three[0], local, incoming, rate, amplitude, long_skip[None], fwd, low, back_start)
    return mixed[None]


def solution(mesh):
    return jax.shard_map(
        body,
        mesh=mesh,
        in_specs=(
            P("dp", "seq", None),
            P("dp", "seq", None),
            P("dp", "seq", None),
            P("dp", "seq", None),
            P("dp", None),
            P(),
            P(None, "dp"),
            P(),
            P(),
            P(),
        ),
        out_specs=P("dp", "seq", None),
        check_vma=False,
    )
```

time: 170 us -> 81.4 us (0.48)
  the two profiles are of different devices: /device:TPU:0 before, /device:TPU:1 now
where the time goes in v1:
time: 81.4 us; the launch traced here: 81.3 us
  Pallas kernels  79.3 us (97%)
  other arithmetic  1.91 us (2%)
    pallas_call x1, Pallas kernels, body(): pl.pallas_call(kernel_states, in_specs=[smem, hbm, hbm, hbm, vmem, vmem,...  55.3 us
    pallas_call x1, Pallas kernels, body(): pl.pallas_call(kernel_mixed, grid=(chunks,), in_specs=[smem, chunked(rows...  24.1 us
    mul x1, other arithmetic, body(): amplitude = residue.T * jnp.sqrt(-jnp.expm1(-2.0 * rate))  1.91 us

profile of v1, /device:TPU:1, one launch (start us, length us, event | category | flops | bytes accessed | tf_op | source)
XLA Modules:
  0.0 81.3 jit_solution(10873768302645896446)
XLA Ops:
  0.0 1.9 %bitcast_multiply_fusion.amplitude_ref = f32[16,4096]{1,0:T(8,128)} fusion(f32[4096,16]{0,1:T(8,128)} %param.22, f32[4096,16]{0,1:T(8,128)} %param.21), kind=kLoop, calls=%fused_computation | loop fusion | flops 196608 | bytes 786432 | tf_op jit(solution)/shard_map/mul | solution.py:397
  1.9 55.3 %states.1 = (bf16[512,4096]{1,0:T(8,128)(2,1)}, f32[4,16,4096]{2,1,0:T(8,128)}, f32[16,16,256]{2,1,0:T(8,128)}) custom-call(s32[1,4]{1,0:T(1,128)} %genome_ref.3, bf16[512,4096]{1,0:T(8,128)(2,1)} %bitcast.11, bf16[512,4096]{1,0:T(8,128)(2,1)} %bitcast.12, bf16[512,4096]{1,0:T(8,128)(2,1)} %bitcast.13, bf16[7,4096]{1,0:T(8,128)(2,1)} %short_ref.1, ...), custom_call_target="tpu_custom_call" | custom-call | tf_op jit(solution)/shard_map/states/pallas_call | solution.py:404
  57.2 24.1 %mixed.1 = bf16[512,4096]{1,0:T(8,128)(2,1)} custom-call(s32[1,4]{1,0:T(1,128)} %genome_ref.3, bf16[512,4096]{1,0:T(8,128)(2,1)} %get-tuple-element.8.second_ref, bf16[512,4096]{1,0:T(8,128)(2,1)} %bitcast.10, f32[4,16,4096]{2,1,0:T(8,128)} %get-tuple-element.9.local_ref, f32[16,16,256]{2,1,0:T(8,128)} %get-tuple-element.10.incoming_ref, ...), custom_call_target="tpu_custom_call" | custom-call | tf_op jit(solution)/shard_map/mixed/pallas_call | solution.py:437

commit v2 on v1

--- a/solution.py
+++ b/solution.py
@@ -16,6 +16,7 @@
 LANES = 128
 F32 = jnp.float32
 BF16 = jnp.bfloat16
+INTRA = F32
 VMEM_LIMIT = 58 * 1024 * 1024
 
 
@@ -46,15 +47,19 @@
     return jnp.dot(a, b, preferred_element_type=F32)
 
 
+def pointwise(spec, product, taps_spec, b):
+    for r in range(0, BLOCK, 16):
+        re, im = slice(r, r + 16), slice(BLOCK + r, BLOCK + r + 16)
+        wr, wi, tr, ti = spec[b, re], spec[b, im], taps_spec(re), taps_spec(im)
+        product[b, re] = (wr * tr - wi * ti).astype(BF16)
+        product[b, im] = (wr * ti + wi * tr).astype(BF16)
+
+
 def staged(fwd_of, signal_of, back, taps_spec, spec, product, blocks):
     for b in blocks:
         spec[b] = dot(fwd_of(b), signal_of(b))
     for b in blocks:
-        for r in range(0, BLOCK, 16):
-            re, im = slice(r, r + 16), slice(BLOCK + r, BLOCK + r + 16)
-            wr, wi, tr, ti = spec[b, re], spec[b, im], taps_spec(re), taps_spec(im)
-            product[b, re] = (wr * tr - wi * ti).astype(BF16)
-            product[b, im] = (wr * ti + wi * tr).astype(BF16)
+        pointwise(spec, product, taps_spec, b)
     return [(b, dot(back, product[b])) for b in blocks]
 
 
@@ -72,6 +77,45 @@
         for k in range(1, SHORT_TAPS):
             total = total + window[tile, 16 - k : 16 - k + BLOCK] * weights[k : k + 1]
         first[rows, lanes] = (gate[rows, lanes].astype(F32) * total).astype(BF16)
+
+
+def sublane_sums(stack):
+    sub = lax.broadcasted_iota(jnp.int32, (8, LANES), 0)
+    groups = []
+    for g in range(0, MODES, 8):
+        level = [stack[g + m] for m in range(8)]
+        for shift in (1, 2, 4):
+            low = (sub & shift) == 0
+            level = [
+                jnp.where(low, a, b) + pltpu.roll(jnp.where(low, b, a), shift, 0)
+                for a, b in zip(level[0::2], level[1::2])
+            ]
+        groups.append(level[0])
+    return jnp.concatenate(groups, axis=0)
+
+
+def long_filter(rate_ref, residue_ref, skip_ref, fwd_ref, low_ref, amplitude_ref, filt, long_spec, i):
+    sub = lax.broadcasted_iota(jnp.int32, (1, 8, 1), 1).astype(F32)
+    for tile in range(WIDE // LANES):
+        own = slice(tile * LANES, (tile + 1) * LANES)
+        lanes = pl.ds(pl.multiple_of(i * WIDE + tile * LANES, LANES), LANES)
+        rate = rate_ref[:, lanes]
+        x = 2.0 * rate
+        series = x * (1.0 - x * (1 / 2) * (1.0 - x * (1 / 3) * (1.0 - x * (1 / 4) * (1.0 - x * (1 / 5)))))
+        amplitude = residue_ref[:, lanes] * jnp.sqrt(jnp.where(x < 0.05, series, 1.0 - jnp.exp(-x)))
+        amplitude_ref[:, lanes] = amplitude
+        rate = rate[:, None, :]
+        step = jnp.broadcast_to(jnp.exp(-8.0 * rate), (MODES, 8, LANES))
+        part = amplitude[:, None, :] * jnp.exp(-sub * rate)
+        for j in range(BLOCK // 8):
+            filt[8 * j : 8 * j + 8, own] = jnp.sum(part, axis=0)
+            part = part * step
+        filt[0:1, own] = filt[0:1, own] + skip_ref[0:1, lanes]
+    taps = filt[...]
+    high = taps.astype(BF16)
+    low = (taps - high.astype(F32)).astype(BF16)
+    lanes = lane_window(i, WIDE)
+    long_spec[:, lanes] = dot(fwd_ref[:, :BLOCK], high) + dot(low_ref[...], high) + dot(fwd_ref[:, :BLOCK], low)
 
 
 def block_states(second, rate_ref, local, blocks, i):
@@ -86,15 +130,16 @@
             acc = jnp.broadcast_to(signal[0:8][None], (MODES, 8, LANES))
             for j in range(1, BLOCK // 8):
                 acc = acc * step + signal[8 * j : 8 * j + 8][None]
-            local[b, :, lanes] = jnp.sum(acc * weight, axis=1)
+            local[b, :, lanes] = sublane_sums(acc * weight)
 
 
 def kernel_states(
-    genome_ref, values_hbm, gate_one_hbm, gate_two_hbm, short_ref, taps_ref, rate_ref, fwd_ref, low_ref, back_ref,
-    second_out, local_out, incoming_out,
+    genome_ref, values_hbm, gate_one_hbm, gate_two_hbm, short_ref, taps_ref, rate_ref, residue_ref, skip_ref, fwd_ref, low_ref,
+    back_ref, back_start_ref,
+    intra_out, local_out, incoming_out, amplitude_out,
     values, gate_one, gate_two, first, second, halo, rim, taps_full, taps_spec, local, ends_own, ends, entering,
-    fwd_keep, window, spec, product,
-    load_sem, store_sem, rim_sem, halo_send, halo_recv, taps_send, taps_recv, ends_send, ends_recv, enter_send, enter_recv,
+    fwd_keep, window, spec, product, amplitude, filt, long_spec, intra,
+    load_sem, store_sem, rim_sem, halo_send, halo_recv, taps_send, taps_recv, ends_send, ends_recv, enter_send, enter_recv, intra_sem,
 ):
     rows, channels = values.shape
     count = rows // BLOCK
@@ -198,6 +243,14 @@
 
     lax.fori_loop(0, chunks, first_step, 0)
 
+    def filter_step(i, carry):
+        long_filter(rate_ref, residue_ref, skip_ref, fwd_ref, low_ref, amplitude, filt, long_spec, i)
+        return carry
+
+    lax.fori_loop(0, chunks, filter_step, 0)
+    store_amplitude = pltpu.make_async_copy(amplitude, amplitude_out, store_sem.at[0])
+    store_amplitude.start()
+
     forwards = []
     for k in range(1, chips):
         source = lax.rem(chip + k, chips) * 2 + core
@@ -226,49 +279,63 @@
         return carry
 
     lax.fori_loop(0, chunks, second_step, 0)
-    late = slice(BLOCK, rows)
-    store_late = pltpu.make_async_copy(second.at[late], second_out.at[late], store_sem.at[0])
-    store_late.start()
-
     def ends_copy(part):
         return remote(ends_own.at[part], ends.at[seq], ends_send.at[part], ends_recv.at[seq], dp, part)
 
-    def opening_step(i, carry):
+    def opening_step(pair, carry):
+        both = [pair * 2, pair * 2 + 1]
+        for h, i in enumerate(both):
+            halo_copy(i).wait_recv()
+        for h, i in enumerate(both):
+            lanes = lane_window(i, WIDE)
+            spec[h] = dot(fwd_keep[0, :, :BLOCK], halo[:, lanes]) + dot(fwd_keep[0, :, BLOCK:], first[0:BLOCK, lanes])
+        for h, i in enumerate(both):
+            lanes = lane_window(i, WIDE)
+            pointwise(spec, product, lambda part: taps_spec[part, lanes], h)
+        for h, i in enumerate(both):
+            lanes = lane_window(i, WIDE)
+            medium = dot(back_ref[...], product[h])
+            second[0:BLOCK, lanes] = (gate_two[0:BLOCK, lanes].astype(F32) * medium).astype(BF16)
+        for i in both:
+            lanes = lane_window(i, WIDE)
+            block_states(second, rate_ref, local, range(1), i)
+            decay = jnp.exp(-float(BLOCK) * rate_ref[:, lanes])
+            total = local[0, :, lanes]
+            for b in range(1, count):
+                total = keeps[b] * decay * total + local[b, :, lanes]
+            for h in range(per_chunk):
+                part = i * per_chunk + h
+                ends_own[part] = total[:, h * width : (h + 1) * width]
+
+                @pl.when(part != seq)
+                def _():
+                    ends_copy(part).start()
+
+                @pl.when(part == seq)
+                def _():
+                    ends[part] = total[:, h * width : (h + 1) * width]
+
+        return carry
+
+    lax.fori_loop(0, chunks // 2, opening_step, 0)
+    store_local = pltpu.make_async_copy(local, local_out, store_sem.at[1])
+    store_local.start()
+
+    def intra_copy(i):
         lanes = lane_window(i, WIDE)
-        halo_copy(i).wait_recv()
-        spec[0] = dot(fwd_keep[0, :, :BLOCK], halo[:, lanes]) + dot(fwd_keep[0, :, BLOCK:], first[0:BLOCK, lanes])
-        for r in range(0, BLOCK, 16):
-            re, im = slice(r, r + 16), slice(BLOCK + r, BLOCK + r + 16)
-            wr, wi, tr, ti = spec[0, re], spec[0, im], taps_spec[re, lanes], taps_spec[im, lanes]
-            product[0, re] = (wr * tr - wi * ti).astype(BF16)
-            product[0, im] = (wr * ti + wi * tr).astype(BF16)
-        medium = dot(back_ref[...], product[0])
-        second[0:BLOCK, lanes] = (gate_two[0:BLOCK, lanes].astype(F32) * medium).astype(BF16)
-        block_states(second, rate_ref, local, range(1), i)
-        decay = jnp.exp(-float(BLOCK) * rate_ref[:, lanes])
-        total = local[0, :, lanes]
-        for b in range(1, count):
-            total = keeps[b] * decay * total + local[b, :, lanes]
-        for h in range(per_chunk):
-            part = i * per_chunk + h
-            ends_own[part] = total[:, h * width : (h + 1) * width]
-
-            @pl.when(part != seq)
-            def _():
-                ends_copy(part).start()
-
-            @pl.when(part == seq)
-            def _():
-                ends[part] = total[:, h * width : (h + 1) * width]
-
-        return carry
-
-    lax.fori_loop(0, chunks, opening_step, 0)
-    early = slice(0, BLOCK)
-    store_early = pltpu.make_async_copy(second.at[early], second_out.at[early], store_sem.at[1])
-    store_early.start()
-    store_local = pltpu.make_async_copy(local, local_out, store_sem.at[2])
-    store_local.start()
+        return pltpu.make_async_copy(intra.at[:, lanes], intra_out.at[:, lanes], intra_sem.at[i])
+
+    def intra_step(i, carry):
+        lanes = lane_window(i, WIDE)
+        for b, result in staged(
+            lambda b: fwd_ref[:, :BLOCK], lambda b: second[b * BLOCK : (b + 1) * BLOCK, lanes], back_start_ref[...],
+            lambda part: long_spec[part, lanes], spec, product, range(count),
+        ):
+            intra[b * BLOCK : (b + 1) * BLOCK, lanes] = result
+        intra_copy(i).start()
+        return carry
+
+    lax.fori_loop(0, chunks // 2, intra_step, 0)
 
     def arrival(k, carry):
         source = lax.rem(seq + k, parts)
@@ -299,7 +366,8 @@
         return through * decay * state + ends[p]
 
     lax.fori_loop(0, parts, scan_step, jnp.zeros((MODES, width), F32))
-    enter_own = pltpu.make_async_copy(entering.at[seq], incoming_out.at[seq], store_sem.at[3])
+    lax.fori_loop(chunks // 2, chunks, intra_step, 0)
+    enter_own = pltpu.make_async_copy(entering.at[seq], incoming_out.at[seq], store_sem.at[2])
     enter_own.start()
 
     def departures(k, carry):
@@ -313,41 +381,21 @@
 
     def halo_sent(i, carry):
         halo_copy(i).wait_send()
+        intra_copy(i).wait()
         return carry
 
     lax.fori_loop(0, chunks, halo_sent, 0)
     for copy in taps_copies + forwards:
         copy.wait_send()
-    for copy in (store_late, store_early, store_local, enter_own):
+    for copy in (store_amplitude, store_local, enter_own):
         copy.wait()
 
 
-def kernel_mixed(
-    genome_ref, second_ref, gate_ref, local_ref, incoming_ref, rate_ref, amplitude_ref, skip_ref, fwd_ref, low_ref, back_ref,
-    mixed_ref, filt, carry, taps_spec, spec, product,
-):
-    count = second_ref.shape[0] // BLOCK
+def kernel_mixed(genome_ref, intra_ref, gate_ref, local_ref, incoming_ref, rate_ref, amplitude_ref, mixed_ref):
+    count = intra_ref.shape[0] // BLOCK
     keeps = keep_scalars(genome_ref, lax.axis_index("seq"), count)
     sub = lax.broadcasted_iota(jnp.int32, (1, 8, 1), 1).astype(F32)
-    pieces, _, width = incoming_ref.shape
-    for tile in range(WIDE // LANES):
-        lanes = slice(tile * LANES, (tile + 1) * LANES)
-        rate = rate_ref[:, lanes]
-        decay = jnp.exp(-float(BLOCK) * rate)
-        rate = rate[:, None, :]
-        step = jnp.broadcast_to(jnp.exp(-8.0 * rate), (MODES, 8, LANES))
-        weight = amplitude_ref[:, lanes][:, None, :] * jnp.exp(-sub * rate)
-        part = weight
-        for j in range(BLOCK // 8):
-            filt[8 * j : 8 * j + 8, lanes] = jnp.sum(part, axis=0)
-            part = part * step
-        filt[0:1, lanes] = filt[0:1, lanes] + skip_ref[0:1, lanes]
-    taps = filt[...]
-    high = taps.astype(BF16)
-    low = (taps - high.astype(F32)).astype(BF16)
-    taps_spec[...] = dot(fwd_ref[:, :BLOCK], high) + dot(low_ref[...], high) + dot(fwd_ref[:, :BLOCK], low)
-    for b in range(count):
-        spec[b] = dot(fwd_ref[:, :BLOCK], second_ref[b * BLOCK : (b + 1) * BLOCK])
+    width = incoming_ref.shape[2]
     for tile in range(WIDE // LANES):
         lanes = slice(tile * LANES, (tile + 1) * LANES)
         rate = rate_ref[:, lanes]
@@ -360,21 +408,16 @@
         for b in range(count):
             state = state * keeps[b]
             part = weight * state[:, None, :]
-            for j in range(BLOCK // 8):
-                carry[b * BLOCK + 8 * j : b * BLOCK + 8 * j + 8, lanes] = jnp.sum(part, axis=0)
+            for j in range(0, BLOCK, 16):
+                rows = slice(b * BLOCK + j, b * BLOCK + j + 16)
+                upper = jnp.sum(part, axis=0)
                 part = part * step
+                lower = jnp.sum(part, axis=0)
+                part = part * step
+                total = intra_ref[rows, lanes].astype(F32) + jnp.concatenate([upper, lower], axis=0)
+                mixed_ref[rows, lanes] = (gate_ref[rows, lanes].astype(F32) * total).astype(BF16)
             if b < count - 1:
                 state = decay * state + local_ref[b, :, lanes]
-    for b in range(count):
-        for r in range(0, BLOCK, 16):
-            re, im = slice(r, r + 16), slice(BLOCK + r, BLOCK + r + 16)
-            wr, wi, tr, ti = spec[b, re], spec[b, im], taps_spec[re], taps_spec[im]
-            product[b, re] = (wr * tr - wi * ti).astype(BF16)
-            product[b, im] = (wr * ti + wi * tr).astype(BF16)
-    for b in range(count):
-        rows = slice(b * BLOCK, (b + 1) * BLOCK)
-        total = dot(back_ref[...], product[b]) + carry[rows]
-        mixed_ref[rows] = (gate_ref[rows].astype(F32) * total).astype(BF16)
 
 
 def chunked(rows):
@@ -394,21 +437,21 @@
     chunks = channels // WIDE
     fwd, low, back_end, back_start = [jnp.asarray(m) for m in transform_matrices()]
     rate = decay_rate.T
-    amplitude = residue.T * jnp.sqrt(-jnp.expm1(-2.0 * rate))
     smem = pl.BlockSpec(memory_space=pltpu.SMEM)
     vmem = pl.BlockSpec(memory_space=pltpu.VMEM)
     hbm = pl.BlockSpec(memory_space=pl.ANY)
     stream = pltpu.VMEM((rows, channels), BF16)
     dma = pltpu.SemaphoreType.DMA
 
-    second, local, incoming = pl.pallas_call(
+    intra, local, incoming, amplitude = pl.pallas_call(
         kernel_states,
-        in_specs=[smem, hbm, hbm, hbm, vmem, vmem, vmem, vmem, vmem, vmem],
-        out_specs=[hbm, hbm, hbm],
+        in_specs=[smem, hbm, hbm, hbm] + [vmem] * 9,
+        out_specs=[hbm] * 4,
         out_shape=[
-            jax.ShapeDtypeStruct((rows, channels), BF16),
+            jax.ShapeDtypeStruct((rows, channels), INTRA),
             jax.ShapeDtypeStruct((count, MODES, channels), F32),
             jax.ShapeDtypeStruct((parts, MODES, width), F32),
+            jax.ShapeDtypeStruct((MODES, channels), F32),
         ],
         scratch_shapes=[
             stream, stream, stream, stream, stream,
@@ -424,14 +467,21 @@
             pltpu.VMEM((WIDE // LANES, 16 + BLOCK, LANES), F32),
             pltpu.VMEM((count, 2 * BLOCK, WIDE), F32),
             pltpu.VMEM((count, 2 * BLOCK, WIDE), BF16),
-            dma((5,)), dma((4,)), dma((2,)), dma((chunks,)), dma((chunks,)), dma((dps,)), dma((dps,)),
-            dma((parts,)), dma((parts,)), dma((parts,)), dma((parts,)),
+            pltpu.VMEM((MODES, channels), F32),
+            pltpu.VMEM((BLOCK, WIDE), F32),
+            pltpu.VMEM((2 * BLOCK, channels), F32),
+            pltpu.VMEM((rows, channels), INTRA),
+            dma((5,)), dma((3,)), dma((2,)), dma((chunks,)), dma((chunks,)), dma((dps,)), dma((dps,)),
+            dma((parts,)), dma((parts,)), dma((parts,)), dma((parts,)), dma((chunks,)),
         ],
         compiler_params=pltpu.CompilerParams(
             vmem_limit_bytes=VMEM_LIMIT, collective_id=0, has_side_effects=True
         ),
         name="states",
-    )(genome_blocks, values[0], gate_one[0], gate_two[0], short_taps, medium_taps, rate, fwd, low, back_end)
+    )(
+        genome_blocks, values[0], gate_one[0], gate_two[0], short_taps, medium_taps, rate, residue.T, long_skip[None],
+        fwd, low, back_end, back_start,
+    )
 
     per_chunk = WIDE // width
     mixed = pl.pallas_call(
@@ -440,21 +490,13 @@
         in_specs=[
             smem, chunked(rows), chunked(rows), pl.BlockSpec((count, MODES, WIDE), lambda i: (0, 0, i)),
             pl.BlockSpec((per_chunk, MODES, width), lambda i: (i, 0, 0)),
-            chunked(MODES), chunked(MODES), chunked(1),
-            whole(fwd.shape), whole(low.shape), whole(back_start.shape),
+            chunked(MODES), chunked(MODES),
         ],
         out_specs=chunked(rows),
         out_shape=jax.ShapeDtypeStruct((rows, channels), BF16),
-        scratch_shapes=[
-            pltpu.VMEM((BLOCK, WIDE), F32),
-            pltpu.VMEM((rows, WIDE), F32),
-            pltpu.VMEM((2 * BLOCK, WIDE), F32),
-            pltpu.VMEM((count, 2 * BLOCK, WIDE), F32),
-            pltpu.VMEM((count, 2 * BLOCK, WIDE), BF16),
-        ],
         compiler_params=pltpu.CompilerParams(vmem_limit_bytes=VMEM_LIMIT),
         name="mixed",
-    )(genome_blocks, second, gate_three[0], local, incoming, rate, amplitude, long_skip[None], fwd, low, back_start)
+    )(genome_blocks, intra, gate_three[0], local, incoming, rate, amplitude)
     return mixed[None]
 
 

time: 81.4 us -> 72.7 us (0.89)
  Pallas kernels: 79.3 us -> 72.3 us
  other arithmetic: 1.91 us -> 0 us
    pallas_call x1, Pallas kernels: 24.1 us -> 14.3 us  [body(): pl.pallas_call(kernel_mixed, grid=(chunks,), in_specs=[smem, chunked(rows...]
    pallas_call x1, Pallas kernels: 55.3 us -> 58 us  [body(): pl.pallas_call(kernel_states, in_specs=[smem, hbm, hbm, hbm] + [vmem] * 9...]
    mul x1 -> x0, other arithmetic: 1.91 us -> none  [body(): amplitude = residue.T * jnp.sqrt(-jnp.expm1(-2.0 * rate))]
where the time goes in v2:
time: 72.7 us; the launch traced here: 72.3 us
  Pallas kernels  72.3 us (99%)
    pallas_call x1, Pallas kernels, body(): pl.pallas_call(kernel_states, in_specs=[smem, hbm, hbm, hbm] + [vmem] * 9...  58 us
    pallas_call x1, Pallas kernels, body(): pl.pallas_call(kernel_mixed, grid=(chunks,), in_specs=[smem, chunked(rows...  14.3 us

profile of v2, /device:TPU:1, one launch (start us, length us, event | category | flops | bytes accessed | tf_op | source)
XLA Modules:
  0.0 72.3 jit_solution(15505433116086649434)
XLA Ops:
  0.0 58.0 %states.1 = (f32[512,4096]{1,0:T(8,128)}, f32[4,16,4096]{2,1,0:T(8,128)}, f32[16,16,256]{2,1,0:T(8,128)}, f32[16,4096]{1,0:T(8,128)}) custom-call(s32[1,4]{1,0:T(1,128)} %genome_ref.3, bf16[512,4096]{1,0:T(8,128)(2,1)} %bitcast.8, bf16[512,4096]{1,0:T(8,128)(2,1)} %bitcast.9, bf16[512,4096]{1,0:T(8,128)(2,1)} %bitcast.10, bf16[7,4096]{1,0:T(8,128)(2,1)} %short_ref.1, ...), custom_call_target="tpu_custom_call" | custom-call | tf_op jit(solution)/shard_map/states/pallas_call | solution.py:446
  58.0 14.3 %mixed.1 = bf16[512,4096]{1,0:T(8,128)(2,1)} custom-call(s32[1,4]{1,0:T(1,128)} %genome_ref.3, f32[512,4096]{1,0:T(8,128)} %get-tuple-element.9.intra_ref, bf16[512,4096]{1,0:T(8,128)(2,1)} %bitcast.11, f32[4,16,4096]{2,1,0:T(8,128)} %get-tuple-element.10.local_ref, f32[16,16,256]{2,1,0:T(8,128)} %get-tuple-element.11.incoming_ref, f32[16,4096]{1,0:T(8,128)} %bitcast.13, ...), custom_call_target="tpu_custom_call" | custom-call | tf_op jit(solution)/shard_map/mixed/pallas_call | solution.py:487

commit v3 on v2

--- a/solution.py
+++ b/solution.py
@@ -28,7 +28,7 @@
     backward = np.concatenate([np.cos(angle).T, -np.sin(angle).T], axis=1) / BLOCK
     high = forward.astype(jnp.bfloat16)
     low = (forward - high.astype(np.float64)).astype(jnp.bfloat16)
-    return high, low[:, :BLOCK], backward[BLOCK:].astype(jnp.bfloat16), backward[:BLOCK].astype(jnp.bfloat16)
+    return high, np.concatenate([high[:, :BLOCK], low[:, :BLOCK]], axis=1), backward[BLOCK:].astype(jnp.bfloat16), backward[:BLOCK].astype(jnp.bfloat16)
 
 
 def keep_scalars(genome_ref, position, count):
@@ -67,15 +67,15 @@
     return pl.ds(pl.multiple_of(i * width, width), width)
 
 
-def short_block(values, before, gate, taps, keep, window, first, rows, i):
+def short_block(values, before, gate, taps, keep, window, slot, first, rows, i):
     for tile in range(WIDE // LANES):
         lanes = pl.ds(pl.multiple_of(i * WIDE + tile * LANES, LANES), LANES)
-        window[tile, 0:16] = before(lanes).astype(F32) * keep
-        window[tile, 16 : 16 + BLOCK] = values[rows, lanes].astype(F32)
+        window[slot + tile, 0:16] = before(lanes).astype(F32) * keep
+        window[slot + tile, 16 : 16 + BLOCK] = values[rows, lanes].astype(F32)
         weights = taps[:, lanes].astype(F32)
-        total = window[tile, 16 : 16 + BLOCK] * weights[0:1]
+        total = window[slot + tile, 16 : 16 + BLOCK] * weights[0:1]
         for k in range(1, SHORT_TAPS):
-            total = total + window[tile, 16 - k : 16 - k + BLOCK] * weights[k : k + 1]
+            total = total + window[slot + tile, 16 - k : 16 - k + BLOCK] * weights[k : k + 1]
         first[rows, lanes] = (gate[rows, lanes].astype(F32) * total).astype(BF16)
 
 
@@ -94,7 +94,7 @@
     return jnp.concatenate(groups, axis=0)
 
 
-def long_filter(rate_ref, residue_ref, skip_ref, fwd_ref, low_ref, amplitude_ref, filt, long_spec, i):
+def long_filter(rate_ref, residue_ref, skip_ref, fwd_ref, pair_ref, amplitude_ref, filt, long_spec, i):
     sub = lax.broadcasted_iota(jnp.int32, (1, 8, 1), 1).astype(F32)
     for tile in range(WIDE // LANES):
         own = slice(tile * LANES, (tile + 1) * LANES)
@@ -115,7 +115,7 @@
     high = taps.astype(BF16)
     low = (taps - high.astype(F32)).astype(BF16)
     lanes = lane_window(i, WIDE)
-    long_spec[:, lanes] = dot(fwd_ref[:, :BLOCK], high) + dot(low_ref[...], high) + dot(fwd_ref[:, :BLOCK], low)
+    long_spec[:, lanes] = dot(pair_ref[...], jnp.concatenate([high, high], axis=0)) + dot(fwd_ref[:, :BLOCK], low)
 
 
 def block_states(second, rate_ref, local, blocks, i):
@@ -134,12 +134,13 @@
 
 
 def kernel_states(
-    genome_ref, values_hbm, gate_one_hbm, gate_two_hbm, short_ref, taps_ref, rate_ref, residue_ref, skip_ref, fwd_ref, low_ref,
-    back_ref, back_start_ref,
+    genome_ref, values_hbm, gate_one_hbm, gate_two_hbm, short_hbm, taps_ref, rate_hbm, residue_hbm, skip_hbm, fwd_hbm, pair_hbm,
+    back_hbm, back_start_hbm,
     intra_out, local_out, incoming_out, amplitude_out,
     values, gate_one, gate_two, first, second, halo, rim, taps_full, taps_spec, local, ends_own, ends, entering,
     fwd_keep, window, spec, product, amplitude, filt, long_spec, intra,
-    load_sem, store_sem, rim_sem, halo_send, halo_recv, taps_send, taps_recv, ends_send, ends_recv, enter_send, enter_recv, intra_sem,
+    short_ref, rate_ref, residue_ref, skip_ref, fwd_ref, pair_ref, back_ref, back_start_ref,
+    small_sem, load_sem, store_sem, rim_sem, halo_send, halo_recv, taps_send, taps_recv, ends_send, ends_recv, enter_send, enter_recv, intra_sem,
 ):
     rows, channels = values.shape
     count = rows // BLOCK
@@ -171,9 +172,21 @@
         (gate_one_hbm, gate_one, slice(0, tail)),
         (gate_two_hbm, gate_two, slice(0, rows)),
     ):
-        copy = pltpu.make_async_copy(src.at[part], dst.at[part], load_sem.at[len(loads)])
+        loads.append(pltpu.make_async_copy(src.at[part], dst.at[part], load_sem.at[len(loads)]))
+    small = [
+        pltpu.make_async_copy(src, dst, small_sem.at[n])
+        for n, (src, dst) in enumerate(
+            (
+                (short_hbm, short_ref), (fwd_hbm, fwd_ref), (rate_hbm, rate_ref), (residue_hbm, residue_ref),
+                (skip_hbm, skip_ref), (pair_hbm, pair_ref), (back_hbm, back_ref), (back_start_hbm, back_start_ref),
+            )
+        )
+    ]
+    small[0].start()
+    loads[0].start()
+    loads[1].start()
+    for copy in small[1:]:
         copy.start()
-        loads.append(copy)
 
     barrier = pltpu.get_barrier_semaphore()
     peers = 0
@@ -205,6 +218,9 @@
 
     loads[0].wait()
     loads[1].wait()
+    small[0].wait()
+    for copy in loads[2:]:
+        copy.start()
 
     def halo_copy(i):
         lanes = lane_window(i, WIDE)
@@ -214,7 +230,7 @@
 
     def tail_step(i, carry):
         short_block(
-            values, lambda lanes: values[tail - 16 : tail, lanes], gate_one, short_ref, keeps[count - 1], window, first,
+            values, lambda lanes: values[tail - 16 : tail, lanes], gate_one, short_ref, keeps[count - 1], window, 0, first,
             slice(tail, rows), i,
         )
         halo_copy(i).start()
@@ -222,10 +238,18 @@
 
     lax.fori_loop(0, chunks, tail_step, 0)
 
+    for copy in small[1:]:
+        copy.wait()
     for b in range(count):
         column = lax.broadcasted_iota(jnp.int32, fwd_ref.shape, 1)
         matrix = fwd_ref[...].astype(F32)
         fwd_keep[b] = jnp.where(column < BLOCK, matrix * keeps[b], matrix).astype(BF16)
+
+    def filter_step(i, carry):
+        long_filter(rate_ref, residue_ref, skip_ref, fwd_ref, pair_ref, amplitude, filt, long_spec, i)
+        return carry
+
+    lax.fori_loop(0, chunks // 2, filter_step, 0)
 
     loads[2].wait()
     loads[3].wait()
@@ -238,18 +262,12 @@
                 before = lambda lanes: rim[:, lanes]
             else:
                 before = lambda lanes, start=start: values[start - 16 : start, lanes]
-            short_block(values, before, gate_one, short_ref, keeps[b], window, first, slice(start, start + BLOCK), i)
+            short_block(
+                values, before, gate_one, short_ref, keeps[b], window, b * (WIDE // LANES), first, slice(start, start + BLOCK), i
+            )
         return carry
 
     lax.fori_loop(0, chunks, first_step, 0)
-
-    def filter_step(i, carry):
-        long_filter(rate_ref, residue_ref, skip_ref, fwd_ref, low_ref, amplitude, filt, long_spec, i)
-        return carry
-
-    lax.fori_loop(0, chunks, filter_step, 0)
-    store_amplitude = pltpu.make_async_copy(amplitude, amplitude_out, store_sem.at[0])
-    store_amplitude.start()
 
     forwards = []
     for k in range(1, chips):
@@ -267,7 +285,7 @@
     def second_step(i, carry):
         lanes = lane_window(i, WIDE)
         taps = taps_full[i]
-        taps_spec[:, lanes] = dot(fwd_ref[:, :BLOCK], taps) + dot(low_ref[...], taps)
+        taps_spec[:, lanes] = dot(pair_ref[...], jnp.concatenate([taps, taps], axis=0))
         blocks = range(1, count)
         for b, medium in staged(
             lambda b: fwd_keep[b], lambda b: first[(b - 1) * BLOCK : (b + 1) * BLOCK, lanes], back_ref[...],
@@ -336,6 +354,7 @@
         return carry
 
     lax.fori_loop(0, chunks // 2, intra_step, 0)
+    lax.fori_loop(chunks // 2, chunks * 3 // 4, filter_step, 0)
 
     def arrival(k, carry):
         source = lax.rem(seq + k, parts)
@@ -366,6 +385,9 @@
         return through * decay * state + ends[p]
 
     lax.fori_loop(0, parts, scan_step, jnp.zeros((MODES, width), F32))
+    lax.fori_loop(chunks * 3 // 4, chunks, filter_step, 0)
+    store_amplitude = pltpu.make_async_copy(amplitude, amplitude_out, store_sem.at[0])
+    store_amplitude.start()
     lax.fori_loop(chunks // 2, chunks, intra_step, 0)
     enter_own = pltpu.make_async_copy(entering.at[seq], incoming_out.at[seq], store_sem.at[2])
     enter_own.start()
@@ -435,17 +457,16 @@
     dps = lax.axis_size("dp")
     width = channels // parts
     chunks = channels // WIDE
-    fwd, low, back_end, back_start = [jnp.asarray(m) for m in transform_matrices()]
+    fwd, pair, back_end, back_start = [jnp.asarray(m) for m in transform_matrices()]
     rate = decay_rate.T
     smem = pl.BlockSpec(memory_space=pltpu.SMEM)
-    vmem = pl.BlockSpec(memory_space=pltpu.VMEM)
     hbm = pl.BlockSpec(memory_space=pl.ANY)
     stream = pltpu.VMEM((rows, channels), BF16)
     dma = pltpu.SemaphoreType.DMA
 
     intra, local, incoming, amplitude = pl.pallas_call(
         kernel_states,
-        in_specs=[smem, hbm, hbm, hbm] + [vmem] * 9,
+        in_specs=[smem] + [hbm] * 12,
         out_specs=[hbm] * 4,
         out_shape=[
             jax.ShapeDtypeStruct((rows, channels), INTRA),
@@ -464,14 +485,22 @@
             pltpu.VMEM((parts, MODES, width), F32),
             pltpu.VMEM((parts, MODES, width), F32),
             pltpu.VMEM((count, 2 * BLOCK, 2 * BLOCK), BF16),
-            pltpu.VMEM((WIDE // LANES, 16 + BLOCK, LANES), F32),
+            pltpu.VMEM((count * (WIDE // LANES), 16 + BLOCK, LANES), F32),
             pltpu.VMEM((count, 2 * BLOCK, WIDE), F32),
             pltpu.VMEM((count, 2 * BLOCK, WIDE), BF16),
             pltpu.VMEM((MODES, channels), F32),
             pltpu.VMEM((BLOCK, WIDE), F32),
             pltpu.VMEM((2 * BLOCK, channels), F32),
             pltpu.VMEM((rows, channels), INTRA),
-            dma((5,)), dma((3,)), dma((2,)), dma((chunks,)), dma((chunks,)), dma((dps,)), dma((dps,)),
+            pltpu.VMEM((SHORT_TAPS, channels), BF16),
+            pltpu.VMEM((MODES, channels), F32),
+            pltpu.VMEM((MODES, channels), F32),
+            pltpu.VMEM((1, channels), F32),
+            pltpu.VMEM(fwd.shape, BF16),
+            pltpu.VMEM(pair.shape, BF16),
+            pltpu.VMEM(back_end.shape, BF16),
+            pltpu.VMEM(back_start.shape, BF16),
+            dma((8,)), dma((5,)), dma((3,)), dma((2,)), dma((chunks,)), dma((chunks,)), dma((dps,)), dma((dps,)),
             dma((parts,)), dma((parts,)), dma((parts,)), dma((parts,)), dma((chunks,)),
         ],
         compiler_params=pltpu.CompilerParams(
@@ -480,7 +509,7 @@
         name="states",
     )(
         genome_blocks, values[0], gate_one[0], gate_two[0], short_taps, medium_taps, rate, residue.T, long_skip[None],
-        fwd, low, back_end, back_start,
+        fwd, pair, back_end, back_start,
     )
 
     per_chunk = WIDE // width

time: 72.7 us -> 68.2 us (0.938)
  Pallas kernels: 72.3 us -> 67.8 us
    pallas_call x1, Pallas kernels: 58 us -> 53.5 us  [body(): pl.pallas_call(kernel_states, in_specs=[smem] + [hbm] * 12, out_specs=[hb...]
where the time goes in v3:
time: 68.2 us; the launch traced here: 67.8 us
  Pallas kernels  67.8 us (99%)
    pallas_call x1, Pallas kernels, body(): pl.pallas_call(kernel_states, in_specs=[smem] + [hbm] * 12, out_specs=[hb...  53.5 us
    pallas_call x1, Pallas kernels, body(): pl.pallas_call(kernel_mixed, grid=(chunks,), in_specs=[smem, chunked(rows...  14.3 us

profile of v3, /device:TPU:1, one launch (start us, length us, event | category | flops | bytes accessed | tf_op | source)
XLA Modules:
  0.0 67.8 jit_solution(13213677840804974100)
XLA Ops:
  0.0 53.5 %states.1 = (f32[512,4096]{1,0:T(8,128)}, f32[4,16,4096]{2,1,0:T(8,128)}, f32[16,16,256]{2,1,0:T(8,128)}, f32[16,4096]{1,0:T(8,128)}) custom-call(s32[1,4]{1,0:T(1,128)} %genome_ref.3, bf16[512,4096]{1,0:T(8,128)(2,1)} %bitcast.8, bf16[512,4096]{1,0:T(8,128)(2,1)} %bitcast.9, bf16[512,4096]{1,0:T(8,128)(2,1)} %bitcast.10, bf16[7,4096]{1,0:T(8,128)(2,1)} %short_hbm.1, ...), custom_call_target="tpu_custom_call" | custom-call | tf_op jit(solution)/shard_map/states/pallas_call | solution.py:467
  53.5 14.3 %mixed.1 = bf16[512,4096]{1,0:T(8,128)(2,1)} custom-call(s32[1,4]{1,0:T(1,128)} %genome_ref.3, f32[512,4096]{1,0:T(8,128)} %get-tuple-element.9.intra_ref, bf16[512,4096]{1,0:T(8,128)(2,1)} %bitcast.11, f32[4,16,4096]{2,1,0:T(8,128)} %get-tuple-element.10.local_ref, f32[16,16,256]{2,1,0:T(8,128)} %get-tuple-element.11.incoming_ref, f32[16,4096]{1,0:T(8,128)} %bitcast.13, ...), custom_call_target="tpu_custom_call" | custom-call | tf_op jit(solution)/shard_map/mixed/pallas_call | solution.py:516

commit v4 on v3

--- a/solution.py
+++ b/solution.py
@@ -16,7 +16,7 @@
 LANES = 128
 F32 = jnp.float32
 BF16 = jnp.bfloat16
-INTRA = F32
+INTRA = BF16
 VMEM_LIMIT = 58 * 1024 * 1024
 
 
@@ -60,7 +60,8 @@
         spec[b] = dot(fwd_of(b), signal_of(b))
     for b in blocks:
         pointwise(spec, product, taps_spec, b)
-    return [(b, dot(back, product[b])) for b in blocks]
+    for b in blocks:
+        yield b, dot(back, product[b])
 
 
 def lane_window(i, width):
@@ -76,7 +77,8 @@
         total = window[slot + tile, 16 : 16 + BLOCK] * weights[0:1]
         for k in range(1, SHORT_TAPS):
             total = total + window[slot + tile, 16 - k : 16 - k + BLOCK] * weights[k : k + 1]
-        first[rows, lanes] = (gate[rows, lanes].astype(F32) * total).astype(BF16)
+        shifted = slice(rows.start + BLOCK, rows.stop + BLOCK)
+        first[shifted, lanes] = (gate[rows, lanes].astype(F32) * total).astype(BF16)
 
 
 def sublane_sums(stack):
@@ -111,11 +113,9 @@
             filt[8 * j : 8 * j + 8, own] = jnp.sum(part, axis=0)
             part = part * step
         filt[0:1, own] = filt[0:1, own] + skip_ref[0:1, lanes]
-    taps = filt[...]
-    high = taps.astype(BF16)
-    low = (taps - high.astype(F32)).astype(BF16)
+    high = filt[...].astype(BF16)
     lanes = lane_window(i, WIDE)
-    long_spec[:, lanes] = dot(pair_ref[...], jnp.concatenate([high, high], axis=0)) + dot(fwd_ref[:, :BLOCK], low)
+    long_spec[:, lanes] = dot(pair_ref[...], jnp.concatenate([high, high], axis=0))
 
 
 def block_states(second, rate_ref, local, blocks, i):
@@ -137,7 +137,7 @@
     genome_ref, values_hbm, gate_one_hbm, gate_two_hbm, short_hbm, taps_ref, rate_hbm, residue_hbm, skip_hbm, fwd_hbm, pair_hbm,
     back_hbm, back_start_hbm,
     intra_out, local_out, incoming_out, amplitude_out,
-    values, gate_one, gate_two, first, second, halo, rim, taps_full, taps_spec, local, ends_own, ends, entering,
+    values, gate_one, gate_two, first, second, rim, taps_full, taps_spec, local, ends_own, ends, entering,
     fwd_keep, window, spec, product, amplitude, filt, long_spec, intra,
     short_ref, rate_ref, residue_ref, skip_ref, fwd_ref, pair_ref, back_ref, back_start_ref,
     small_sem, load_sem, store_sem, rim_sem, halo_send, halo_recv, taps_send, taps_recv, ends_send, ends_recv, enter_send, enter_recv, intra_sem,
@@ -225,7 +225,7 @@
     def halo_copy(i):
         lanes = lane_window(i, WIDE)
         return remote(
-            first.at[slice(tail, rows), lanes], halo.at[:, lanes], halo_send.at[i], halo_recv.at[i], dp, following
+            first.at[slice(rows, rows + BLOCK), lanes], first.at[slice(0, BLOCK), lanes], halo_send.at[i], halo_recv.at[i], dp, following
         )
 
     def tail_step(i, carry):
@@ -288,7 +288,7 @@
         taps_spec[:, lanes] = dot(pair_ref[...], jnp.concatenate([taps, taps], axis=0))
         blocks = range(1, count)
         for b, medium in staged(
-            lambda b: fwd_keep[b], lambda b: first[(b - 1) * BLOCK : (b + 1) * BLOCK, lanes], back_ref[...],
+            lambda b: fwd_keep[b], lambda b: first[b * BLOCK : (b + 2) * BLOCK, lanes], back_ref[...],
             lambda part: taps_spec[part, lanes], spec, product, blocks,
         ):
             part = slice(b * BLOCK, (b + 1) * BLOCK)
@@ -306,7 +306,7 @@
             halo_copy(i).wait_recv()
         for h, i in enumerate(both):
             lanes = lane_window(i, WIDE)
-            spec[h] = dot(fwd_keep[0, :, :BLOCK], halo[:, lanes]) + dot(fwd_keep[0, :, BLOCK:], first[0:BLOCK, lanes])
+            spec[h] = dot(fwd_keep[0], first[0 : 2 * BLOCK, lanes])
         for h, i in enumerate(both):
             lanes = lane_window(i, WIDE)
             pointwise(spec, product, lambda part: taps_spec[part, lanes], h)
@@ -349,7 +349,7 @@
             lambda b: fwd_ref[:, :BLOCK], lambda b: second[b * BLOCK : (b + 1) * BLOCK, lanes], back_start_ref[...],
             lambda part: long_spec[part, lanes], spec, product, range(count),
         ):
-            intra[b * BLOCK : (b + 1) * BLOCK, lanes] = result
+            intra[b * BLOCK : (b + 1) * BLOCK, lanes] = result.astype(INTRA)
         intra_copy(i).start()
         return carry
 
@@ -475,8 +475,9 @@
             jax.ShapeDtypeStruct((MODES, channels), F32),
         ],
         scratch_shapes=[
-            stream, stream, stream, stream, stream,
-            pltpu.VMEM((BLOCK, channels), BF16),
+            stream, stream, stream,
+            pltpu.VMEM((rows + BLOCK, channels), BF16),
+            stream,
             pltpu.VMEM((16, channels), BF16),
             pltpu.VMEM((dps, BLOCK, WIDE), BF16),
             pltpu.VMEM((2 * BLOCK, channels), F32),

time: 68.2 us -> 67 us (0.982)
  Pallas kernels: 67.8 us -> 66.8 us
    pallas_call x1, Pallas kernels: 53.5 us -> 52.8 us  [body(): pl.pallas_call(kernel_states, in_specs=[smem] + [hbm] * 12, out_specs=[hb...]
where the time goes in v4:
time: 67 us; the launch traced here: 66.8 us
  Pallas kernels  66.8 us (100%)
    pallas_call x1, Pallas kernels, body(): pl.pallas_call(kernel_states, in_specs=[smem] + [hbm] * 12, out_specs=[hb...  52.8 us
    pallas_call x1, Pallas kernels, body(): pl.pallas_call(kernel_mixed, grid=(chunks,), in_specs=[smem, chunked(rows...  13.9 us

profile of v4, /device:TPU:1, one launch (start us, length us, event | category | flops | bytes accessed | tf_op | source)
XLA Modules:
  0.0 66.8 jit_solution(7149120409427641687)
XLA Ops:
  0.0 52.8 %states.1 = (bf16[512,4096]{1,0:T(8,128)(2,1)}, f32[4,16,4096]{2,1,0:T(8,128)}, f32[16,16,256]{2,1,0:T(8,128)}, f32[16,4096]{1,0:T(8,128)}) custom-call(s32[1,4]{1,0:T(1,128)} %genome_ref.3, bf16[512,4096]{1,0:T(8,128)(2,1)} %bitcast.8, bf16[512,4096]{1,0:T(8,128)(2,1)} %bitcast.9, bf16[512,4096]{1,0:T(8,128)(2,1)} %bitcast.10, bf16[7,4096]{1,0:T(8,128)(2,1)} %short_hbm.1, ...), custom_call_target="tpu_custom_call" | custom-call | tf_op jit(solution)/shard_map/states/pallas_call | solution.py:467
  52.8 13.9 %mixed.1 = bf16[512,4096]{1,0:T(8,128)(2,1)} custom-call(s32[1,4]{1,0:T(1,128)} %genome_ref.3, bf16[512,4096]{1,0:T(8,128)(2,1)} %get-tuple-element.9.intra_ref, bf16[512,4096]{1,0:T(8,128)(2,1)} %bitcast.11, f32[4,16,4096]{2,1,0:T(8,128)} %get-tuple-element.10.local_ref, f32[16,16,256]{2,1,0:T(8,128)} %get-tuple-element.11.incoming_ref, ...), custom_call_target="tpu_custom_call" | custom-call | tf_op jit(solution)/shard_map/mixed/pallas_call | solution.py:517

commit v5 on v4

--- a/solution.py
+++ b/solution.py
@@ -249,7 +249,7 @@
         long_filter(rate_ref, residue_ref, skip_ref, fwd_ref, pair_ref, amplitude, filt, long_spec, i)
         return carry
 
-    lax.fori_loop(0, chunks // 2, filter_step, 0)
+    lax.fori_loop(0, chunks * 3 // 4, filter_step, 0)
 
     loads[2].wait()
     loads[3].wait()
@@ -301,7 +301,7 @@
         return remote(ends_own.at[part], ends.at[seq], ends_send.at[part], ends_recv.at[seq], dp, part)
 
     def opening_step(pair, carry):
-        both = [pair * 2, pair * 2 + 1]
+        both = [pair * 4 + n for n in range(4)]
         for h, i in enumerate(both):
             halo_copy(i).wait_recv()
         for h, i in enumerate(both):
@@ -335,7 +335,7 @@
 
         return carry
 
-    lax.fori_loop(0, chunks // 2, opening_step, 0)
+    lax.fori_loop(0, chunks // 4, opening_step, 0)
     store_local = pltpu.make_async_copy(local, local_out, store_sem.at[1])
     store_local.start()
 
@@ -354,7 +354,6 @@
         return carry
 
     lax.fori_loop(0, chunks // 2, intra_step, 0)
-    lax.fori_loop(chunks // 2, chunks * 3 // 4, filter_step, 0)
 
     def arrival(k, carry):
         source = lax.rem(seq + k, parts)

time: 67 us -> 65.1 us (0.972)
  Pallas kernels: 66.8 us -> 64.9 us
    pallas_call x1, Pallas kernels: 52.8 us -> 51 us  [body(): pl.pallas_call(kernel_states, in_specs=[smem] + [hbm] * 12, out_specs=[hb...]
where the time goes in v5:
time: 65.1 us; the launch traced here: 64.9 us
  Pallas kernels  64.9 us (100%)
    pallas_call x1, Pallas kernels, body(): pl.pallas_call(kernel_states, in_specs=[smem] + [hbm] * 12, out_specs=[hb...  51 us
    pallas_call x1, Pallas kernels, body(): pl.pallas_call(kernel_mixed, grid=(chunks,), in_specs=[smem, chunked(rows...  13.9 us

profile of v5, /device:TPU:1, one launch (start us, length us, event | category | flops | bytes accessed | tf_op | source)
XLA Modules:
  0.0 64.9 jit_solution(8612113280787223683)
XLA Ops:
  0.0 51.0 %states.1 = (bf16[512,4096]{1,0:T(8,128)(2,1)}, f32[4,16,4096]{2,1,0:T(8,128)}, f32[16,16,256]{2,1,0:T(8,128)}, f32[16,4096]{1,0:T(8,128)}) custom-call(s32[1,4]{1,0:T(1,128)} %genome_ref.3, bf16[512,4096]{1,0:T(8,128)(2,1)} %bitcast.8, bf16[512,4096]{1,0:T(8,128)(2,1)} %bitcast.9, bf16[512,4096]{1,0:T(8,128)(2,1)} %bitcast.10, bf16[7,4096]{1,0:T(8,128)(2,1)} %short_hbm.1, ...), custom_call_target="tpu_custom_call" | custom-call | tf_op jit(solution)/shard_map/states/pallas_call | solution.py:466
  51.0 13.9 %mixed.1 = bf16[512,4096]{1,0:T(8,128)(2,1)} custom-call(s32[1,4]{1,0:T(1,128)} %genome_ref.3, bf16[512,4096]{1,0:T(8,128)(2,1)} %get-tuple-element.9.intra_ref, bf16[512,4096]{1,0:T(8,128)(2,1)} %bitcast.11, f32[4,16,4096]{2,1,0:T(8,128)} %get-tuple-element.10.local_ref, f32[16,16,256]{2,1,0:T(8,128)} %get-tuple-element.11.incoming_ref, ...), custom_call_target="tpu_custom_call" | custom-call | tf_op jit(solution)/shard_map/mixed/pallas_call | solution.py:516

commit v6 on v5

--- a/solution.py
+++ b/solution.py
@@ -249,7 +249,7 @@
         long_filter(rate_ref, residue_ref, skip_ref, fwd_ref, pair_ref, amplitude, filt, long_spec, i)
         return carry
 
-    lax.fori_loop(0, chunks * 3 // 4, filter_step, 0)
+    lax.fori_loop(0, chunks, filter_step, 0)
 
     loads[2].wait()
     loads[3].wait()
@@ -384,7 +384,6 @@
         return through * decay * state + ends[p]
 
     lax.fori_loop(0, parts, scan_step, jnp.zeros((MODES, width), F32))
-    lax.fori_loop(chunks * 3 // 4, chunks, filter_step, 0)
     store_amplitude = pltpu.make_async_copy(amplitude, amplitude_out, store_sem.at[0])
     store_amplitude.start()
     lax.fori_loop(chunks // 2, chunks, intra_step, 0)

time: 65.1 us -> 65.5 us (level)
  no operation moved by 1% of the time
where the time goes in v6:
time: 65.5 us; the launch traced here: 65.3 us
  Pallas kernels  65.3 us (100%)
    pallas_call x1, Pallas kernels, body(): pl.pallas_call(kernel_states, in_specs=[smem] + [hbm] * 12, out_specs=[hb...  51.3 us
    pallas_call x1, Pallas kernels, body(): pl.pallas_call(kernel_mixed, grid=(chunks,), in_specs=[smem, chunked(rows...  13.9 us

profile of v6, /device:TPU:1, one launch (start us, length us, event | category | flops | bytes accessed | tf_op | source)
XLA Modules:
  0.0 65.3 jit_solution(12283430480284878615)
XLA Ops:
  0.0 51.3 %states.1 = (bf16[512,4096]{1,0:T(8,128)(2,1)}, f32[4,16,4096]{2,1,0:T(8,128)}, f32[16,16,256]{2,1,0:T(8,128)}, f32[16,4096]{1,0:T(8,128)}) custom-call(s32[1,4]{1,0:T(1,128)} %genome_ref.3, bf16[512,4096]{1,0:T(8,128)(2,1)} %bitcast.8, bf16[512,4096]{1,0:T(8,128)(2,1)} %bitcast.9, bf16[512,4096]{1,0:T(8,128)(2,1)} %bitcast.10, bf16[7,4096]{1,0:T(8,128)(2,1)} %short_hbm.1, ...), custom_call_target="tpu_custom_call" | custom-call | tf_op jit(solution)/shard_map/states/pallas_call | solution.py:465
  51.3 13.9 %mixed.1 = bf16[512,4096]{1,0:T(8,128)(2,1)} custom-call(s32[1,4]{1,0:T(1,128)} %genome_ref.3, bf16[512,4096]{1,0:T(8,128)(2,1)} %get-tuple-element.9.intra_ref, bf16[512,4096]{1,0:T(8,128)(2,1)} %bitcast.11, f32[4,16,4096]{2,1,0:T(8,128)} %get-tuple-element.10.local_ref, f32[16,16,256]{2,1,0:T(8,128)} %get-tuple-element.11.incoming_ref, ...), custom_call_target="tpu_custom_call" | custom-call | tf_op jit(solution)/shard_map/mixed/pallas_call | solution.py:515
